TPU v7x, 32 devices: a whole 2x2x4 slice. The times are simulated.
32 devices in a mesh: block: 8 (over z, x), grp: 4 (over y, core).
Axes of the slice: x: 2, y: 2, z: 4, core: 2. Of those that a mesh axis runs over, the one named last changes fastest.
Arguments:
- features: bfloat16 [128, 256, 128], P(('block', 'grp')), may hold values from -6 to 6
- point_counts: int32 [128], P(('block', 'grp')), may hold values from 128 to 256, as said below
- kernel_weights: bfloat16 [15, 128, 128], replicated, may hold values from -0.015625 to 0.015625
- influence: bfloat16 [256, 15, 256, 256], P(('block', 'grp')), may hold values from 0 to 1
- pair_list: int32 [256, 2], P(('block', 'grp')), may hold values from 0 to 127, as said below
- pair_counts: int32 [32], P(('block', 'grp')), may hold values from 1 to 8, as said below
- cotangent: bfloat16 [128, 256, 128], P(('block', 'grp')), may hold values from -6 to 6
Outputs:
- activated: bfloat16 [128, 256, 128], P(('block', 'grp'))
- grad_features: bfloat16 [128, 256, 128], P(('block', 'grp'))
- grad_weights: float32 [15, 128, 128], replicated
Inputs may be any that keep to these rules, and one draw needn't show every extreme that they name: `pair_list`: block x lives on device x // 4, and device d has block index d // 4 and grp index d % 4. Column 0 is below 4; the second block of every slot lives on a device whose block index differs from the slot's device's by at most one; any grp index may occur. `pair_counts`: slots at or beyond a device's count are unused. Some device uses all 8 slots. `point_counts`: the real points of a block are its first rows; the others are padding.
All inputs are finite; a program needn't handle non-finite values.
Results may differ from a plain program's by a relative error of at most 0.0063.
Values may be sent and summed in bfloat16 or wider, within the bound.
A program may use at most 128 MiB of HBM per device.

v0:
```python
import math

import jax
import jax.numpy as jnp
from jax import lax
from jax.sharding import PartitionSpec as P


def with_halo(array, sides, width):
    for axis, dim in sides:
        peers, length = (lax.axis_size(axis), array.shape[dim])
        up = [(i, (i + 1) % peers) for i in range(peers - 1)]
        down = [(j, i) for i, j in up]
        last = lax.slice_in_dim(array, length - width, length, axis=dim)
        initial = lax.slice_in_dim(array, 0, width, axis=dim)
        before = lax.ppermute(last, axis, up)
        after = lax.ppermute(initial, axis, down)
        array = jnp.concatenate([before, array, after], axis=dim)
    return array


def shifted(block, axis, distance):
    devices = range(lax.axis_size(axis))
    route = [(i - distance, i) for i in devices if i - distance in devices]
    return lax.ppermute(block, axis, route)


def gather_terms(tile, rows):
    out = jnp.einsum("kij,jc->ikc", tile, rows, preferred_element_type=jnp.float32)
    return out.astype(jnp.bfloat16).reshape(rows.shape[0], -1)


def scatter_terms(tile, rows):
    out = jnp.einsum("kij,ic->jkc", tile, rows, preferred_element_type=jnp.float32)
    return out.astype(jnp.bfloat16).reshape(rows.shape[0], -1)


def neighbours(values):
    region = lax.all_gather(values, "grp", axis=0, tiled=True)
    return with_halo(region[None], (("block", 0),), 1)


def collect(partial_value):
    from_lower = shifted(partial_value[2], "block", 1)
    from_upper = shifted(partial_value[0], "block", -1)
    return lax.psum_scatter(
        partial_value[1] + from_lower + from_upper, "grp", scatter_dimension=0, tiled=True
    )


def body(features, point_counts, kernel_weights, influence, pair_list, pair_counts, cotangent):
    block_count, points, width = features.shape
    kernels = kernel_weights.shape[0]
    slot_count = influence.shape[0]
    regions = lax.axis_size("grp")
    column_here = lax.axis_index("block")
    valid = (lax.broadcasted_iota(jnp.int32, (block_count, points), 1) < point_counts[:, None])[
        ..., None
    ]
    masked = jnp.where(valid, features, jnp.zeros_like(features))
    direct = kernel_weights.reshape(kernels * width, width)
    mirrored = kernel_weights[::-1].reshape(kernels * width, width)
    used = pair_counts[0]

    def locate(slot):
        pair = pair_list[slot]
        second = pair[1]
        owner = second // block_count
        column = owner // regions - column_here + 1
        row_index = owner % regions * block_count + second % block_count
        return (pair[0], column, row_index)

    near_rows = neighbours(masked)
    own_zero = jnp.zeros((block_count, points, width), jnp.float32)
    sent_zero = jnp.zeros((3, regions * block_count, points, width), jnp.float32)
    store_zero = jnp.zeros((slot_count, points, kernels * width), jnp.bfloat16)

    def forward_pair(slot, carry):
        own_total, sent, near_store, own_store = carry
        first, column, row_index = locate(slot)
        tile = influence[slot]
        near_terms = gather_terms(tile, near_rows[column, row_index])
        own_terms = scatter_terms(tile, masked[first])
        to_first = jnp.dot(near_terms, direct, preferred_element_type=jnp.float32)
        to_second = jnp.dot(own_terms, mirrored, preferred_element_type=jnp.float32)
        own_total = own_total.at[first].add(to_first)
        sent = sent.at[column, row_index].add(to_second)
        near_store = lax.dynamic_update_index_in_dim(near_store, near_terms, slot, 0)
        own_store = lax.dynamic_update_index_in_dim(own_store, own_terms, slot, 0)
        return (own_total, sent, near_store, own_store)

    own_total, sent, near_store, own_store = lax.fori_loop(
        0, used, forward_pair, (own_zero, sent_zero, store_zero, store_zero)
    )
    summed = own_total + collect(sent)
    pre = jnp.where(valid, summed, jnp.zeros_like(summed))
    activated = jax.nn.silu(pre).astype(jnp.bfloat16)
    sig = jax.nn.sigmoid(pre)
    slope = sig * (1.0 + pre * (1.0 - sig))
    upstream = jnp.where(valid, cotangent.astype(jnp.float32) * slope, jnp.zeros_like(pre)).astype(
        jnp.bfloat16
    )
    near_upstream = neighbours(upstream)
    weight_zero = jnp.zeros((kernels * width, width), jnp.float32)

    def backward_pair(slot, carry):
        own_grad, sent_grad, grad_direct, grad_mirror = carry
        first, column, row_index = locate(slot)
        tile = influence[slot]
        near_terms = near_store[slot]
        own_terms = own_store[slot]
        up_first = upstream[first]
        up_second = near_upstream[column, row_index]
        grad_direct = grad_direct + jnp.einsum(
            "pr,pe->re", near_terms, up_first, preferred_element_type=jnp.float32
        )
        grad_mirror = grad_mirror + jnp.einsum(
            "pr,pe->re", own_terms, up_second, preferred_element_type=jnp.float32
        )
        back_near = jnp.einsum("pe,re->pr", up_first, direct, preferred_element_type=jnp.float32)
        back_near = back_near.astype(jnp.bfloat16).reshape(points, kernels, width)
        back_own = jnp.einsum("pe,re->pr", up_second, mirrored, preferred_element_type=jnp.float32)
        back_own = back_own.astype(jnp.bfloat16).reshape(points, kernels, width)
        to_second = jnp.einsum("kij,ikc->jc", tile, back_near, preferred_element_type=jnp.float32)
        to_first = jnp.einsum("kij,jkc->ic", tile, back_own, preferred_element_type=jnp.float32)
        own_grad = own_grad.at[first].add(to_first)
        sent_grad = sent_grad.at[column, row_index].add(to_second)
        return (own_grad, sent_grad, grad_direct, grad_mirror)

    own_grad, sent_grad, grad_direct, grad_mirror = lax.fori_loop(
        0, used, backward_pair, (own_zero, sent_zero, weight_zero, weight_zero)
    )
    grad_rows = own_grad + collect(sent_grad)
    grad_features = jnp.where(valid, grad_rows, jnp.zeros_like(grad_rows)).astype(jnp.bfloat16)
    local_weights = (
        grad_direct.reshape(kernels, width, width)
        + grad_mirror.reshape(kernels, width, width)[::-1]
    )
    total_weights = lax.psum(local_weights, ("block", "grp"))
    total_points = block_count * points * lax.axis_size("block") * regions
    grad_weights = total_weights * (1.0 / math.sqrt(total_points))
    return (activated, grad_features, grad_weights)


def solution(mesh):
    placed = (
        P(("block", "grp"), None, None),
        P(("block", "grp")),
        P(),
        P(("block", "grp"), None, None, None),
        P(("block", "grp"), None),
        P(("block", "grp")),
        P(("block", "grp"), None, None),
    )
    return jax.shard_map(
        body,
        mesh=mesh,
        in_specs=placed,
        out_specs=(P(("block", "grp"), None, None), P(("block", "grp"), None, None), P()),
        check_vma=False,
    )
```

profile of v0, /device:TPU:0, one launch (start us, length us, event | category | flops | bytes accessed | tf_op | source)
XLA Modules:
  0.0 788.7 jit_solution(8071054446670976603)
XLA Ops:
  9.9 19.7 %all-gather.3.cloned.1.call-done = bf16[16,256,128]{2,1,0:T(8,128)(2,1)} async-done(((bf16[4,256,128]{2,1,0:T(8,128)(2,1)}), bf16[16,256,128]{2,1,0:T(8,128)(2,1)}) %all-gather.3.cloned.1.call-update) | async-done | bytes 1048592 | tf_op jit(solution)/shard_map/all_gather | solution.py:39
  29.6 3.4 collective-permute-start
  35.4 43.1 %collective-permute-done = bf16[1,16,256,128]{3,2,1,0:T(8,128)(2,1)S(1)} collective-permute-done((bf16[1,16,256,128]{3,2,1,0:T(8,128)(2,1)}, bf16[1,16,256,128]{3,2,1,0:T(8,128)(2,1)S(1)}, u32[]{:S(2)}, u32[]{:S(2)}) %collective-permute-start) | collective-permute-done | bytes 1048608 | tf_op jit(solution)/shard_map/ppermute | solution.py:16
  78.5 3.2 pad_maximum_fusion
  81.8 3.5 broadcast_in_dim.79
  85.3 3.7 broadcast_in_dim.79.clone
  89.0 3.4 broadcast_in_dim.78.clone
  92.5 85.3 %while.42 = (s32[]{:T(128)}, f32[4,256,128]{2,1,0:T(8,128)S(1)}, f32[3,16,256,128]{3,2,1,0:T(8,128)}, bf16[8,256,1920]{1,2,0:T(8,128)(2,1)}, bf16[8,256,1920]{1,...) while((s32[]{:T(128)}, f32[4,256,128]{2,1,0:T(8,128)S(1)}, ...), condition=%wide.region_3.4_spmd, body=%wide.region_0.3_spmd.sunk | while | flops 756088896 | bytes 13438826 | solution.py:92
  96.4 2.4 fusion.121
  105.0 2.7 fusion.124
  121.9 2.7 fusion.124
  130.3 2.4 fusion.121
  138.8 2.7 fusion.124
  147.2 2.4 fusion.121
  155.8 2.7 fusion.124
  172.7 2.7 fusion.124
  177.8 2.5 slice_bitcast_fusion.3
  180.3 4.4 collective-permute-start.2
  186.2 70.9 %collective-permute-done.2 = f32[16,256,128]{2,1,0:T(8,128)S(1)} collective-permute-done((f32[16,256,128]{2,1,0:T(8,128)S(1)}, f32[16,256,128]{2,1,0:T(8,128)S(1)}, u32[]{:S(2)}, u32[]{:S(2)}) %collective-permute-start.2) | collective-permute-done | bytes 2097184 | tf_op jit(solution)/shard_map/ppermute | solution.py:25
  257.1 3.3 fusion.73
  260.4 76.4 %reduce-scatter.3.cloned.1.call-done = f32[4,256,128]{2,1,0:T(8,128)} async-done(((f32[16,256,128]{2,1,0:T(8,128)}), f32[4,256,128]{2,1,0:T(8,128)}) %reduce-scatter.3.cloned.1.call-update) | async-done | bytes 524304 | tf_op jit(solution)/shard_map/reduce_scatter | solution.py:46
  339.0 16.8 %all-gather.5.cloned.1.call-done = bf16[16,256,128]{2,1,0:T(8,128)(2,1)} async-done(((bf16[4,256,128]{2,1,0:T(8,128)(2,1)}), bf16[16,256,128]{2,1,0:T(8,128)(2,1)}) %all-gather.5.cloned.1.call-update) | async-done | bytes 1048592 | tf_op jit(solution)/shard_map/all_gather | solution.py:39
  355.8 3.4 collective-permute-start.4
  360.6 44.2 %collective-permute-done.4 = bf16[1,16,256,128]{3,2,1,0:T(8,128)(2,1)S(1)} collective-permute-done((bf16[1,16,256,128]{3,2,1,0:T(8,128)(2,1)}, bf16[1,16,256,128]{3,2,1,0:T(8,128)(2,1)S(1)}, u32[]{:S(2)}, u32[]{:S(2)}) %collective-permute-start.4) | collective-permute-done | bytes 1048608 | tf_op jit(solution)/shard_map/ppermute | solution.py:16
  404.8 3.2 pad_maximum_fusion.1
  408.0 3.4 broadcast_in_dim.78
  413.6 112.3 %while.43 = (s32[]{:T(128)}, f32[4,256,128]{2,1,0:T(8,128)S(1)}, f32[3,16,256,128]{3,2,1,0:T(8,128)}, f32[1920,128]{1,0:T(8,128)}, f32[1920,128]{1,0:T(8,128)}, ...) while((s32[]{:T(128)}, f32[4,256,128]{2,1,0:T(8,128)S(1)}, ...), condition=%wide.region_8.9_spmd, body=%wide.region_5.8_spmd.sunk | while | flops 1008238720 | bytes 27335088 | solution.py:130
  421.9 3.6 fusion.139
  428.2 2.8 fusion.138
  432.7 3.3 convolution_add_fusion.4
  444.3 3.6 fusion.139
  450.5 2.8 fusion.138
  455.0 3.3 convolution_add_fusion.4
  466.6 3.6 fusion.139
  472.8 2.8 fusion.138
  477.3 3.3 convolution_add_fusion.4
  488.9 3.6 fusion.139
  495.2 2.8 fusion.138
  499.6 3.3 convolution_add_fusion.4
  511.2 3.6 fusion.139
  517.5 2.8 fusion.138
  522.0 3.3 convolution_add_fusion.4
  525.9 4.7 slice_bitcast_fusion.1
  530.6 5.6 collective-permute-start.6
  539.9 63.8 %collective-permute-done.6 = f32[16,256,128]{2,1,0:T(8,128)} collective-permute-done((f32[16,256,128]{2,1,0:T(8,128)}, f32[16,256,128]{2,1,0:T(8,128)}, u32[]{:S(2)}, u32[]{:S(2)}) %collective-permute-start.6) | collective-permute-done | bytes 2097184 | tf_op jit(solution)/shard_map/ppermute | solution.py:25
  603.7 4.6 fusion.72
  608.3 138.1 %all-reduce.2.cloned.1.call-done = f32[15,128,128]{2,1,0:T(8,128)} async-done(((f32[15,128,128]{2,1,0:T(8,128)}), f32[15,128,128]{2,1,0:T(8,128)}) %all-reduce.2.cloned.1.call-update) | async-done | bytes 983056 | tf_op jit(solution)/shard_map/psum | solution.py:139
  748.6 31.6 %reduce-scatter.5.cloned.1.call-done = f32[4,256,128]{2,1,0:T(8,128)} async-done(((f32[16,256,128]{2,1,0:T(8,128)}), f32[4,256,128]{2,1,0:T(8,128)}) %reduce-scatter.5.cloned.1.call-update) | async-done | bytes 524304 | tf_op jit(solution)/shard_map/reduce_scatter | solution.py:46
  (143 shorter events, 96.2 us)
Async XLA Ops:
  7.2 22.4 %all-gather.3.cloned.1.call-start = ((), (), s32[]{:S(2)}) async-start(), calls=%async_computation.2 | async-start | bytes 1310720 | tf_op jit(solution)/shard_map/all_gather | solution.py:39
  9.8 326.9 %reduce-scatter.3.cloned.1.call-start = ((), (), s32[]{:S(2)}) async-start(), calls=%async_computation.3 | async-start | bytes 2621440 | tf_op jit(solution)/shard_map/reduce_scatter | solution.py:46
  29.6 49.0 %collective-permute-start = (bf16[1,16,256,128]{3,2,1,0:T(8,128)(2,1)}, bf16[1,16,256,128]{3,2,1,0:T(8,128)(2,1)S(1)}, u32[]{:S(2)}, u32[]{:S(2)}) collective-permute-start(bf16[1,16,256,128]{3,2,1,0:T(8,128)(2,1)} %bitcast.236), channel_id=1, source_target_pairs={{0,4},{4,8},{8,12},{12,16},{16,20},{20,24},{24,28},{1,5},{5,9},{9,... | collective-permute-start | bytes 3145736 | tf_op jit(solution)/shard_map/ppermute | solution.py:16
  33.0 45.5 %collective-permute-start.1 = (bf16[1,16,256,128]{3,2,1,0:T(8,128)(2,1)}, bf16[1,16,256,128]{3,2,1,0:T(8,128)(2,1)S(1)}, u32[]{:S(2)}, u32[]{:S(2)}) collective-permute-start(bf16[1,16,256,128]{3,2,1,0:T(8,128)(2,1)} %bitcast.237), channel_id=1, source_target_pairs={{4,0},{8,4},{12,8},{16,12},{20,16},{24,20},{28,24},{5,1},{9,5},{13... | collective-permute-start | bytes 3145736 | tf_op jit(solution)/shard_map/ppermute | solution.py:17
  89.0 3.4 copy-start
  89.0 3.4 copy-start.5
  89.0 3.5 copy-start.6
  89.0 3.5 copy-start.7
  180.3 76.7 %collective-permute-start.2 = (f32[16,256,128]{2,1,0:T(8,128)S(1)}, f32[16,256,128]{2,1,0:T(8,128)S(1)}, u32[]{:S(2)}, u32[]{:S(2)}) collective-permute-start(f32[16,256,128]{2,1,0:T(8,128)S(1)} %get-tuple-element.659), channel_id=1, source_target_pairs={{0,4},{4,8},{8,12},{12,16},{16,20},{20,24},{24,28},{1,5},{5,9},{9,... | collective-permute-start | bytes 6291464 | tf_op jit(solution)/shard_map/ppermute | solution.py:25
  184.7 152.0 %copy-start.4 = (bf16[4,256,128]{2,1,0:T(8,128)(2,1)S(1)}, bf16[4,256,128]{2,1,0:T(8,128)(2,1)}, u32[]{:S(2)}) copy-start(bf16[4,256,128]{2,1,0:T(8,128)(2,1)} %param.25) | copy-start | bytes 786436
  184.8 72.3 %collective-permute-start.3 = (f32[16,256,128]{2,1,0:T(8,128)S(1)}, f32[16,256,128]{2,1,0:T(8,128)S(1)}, u32[]{:S(2)}, u32[]{:S(2)}) collective-permute-start(f32[16,256,128]{2,1,0:T(8,128)S(1)} %get-tuple-element.660), channel_id=1, source_target_pairs={{4,0},{8,4},{12,8},{16,12},{20,16},{24,20},{28,24},{5,1},{9,5},{13... | collective-permute-start | bytes 6291464 | tf_op jit(solution)/shard_map/ppermute | solution.py:25
  260.4 95.5 %all-gather.5.cloned.1.call-start = ((), (), s32[]{:S(2)}) async-start(), calls=%async_computation.4 | async-start | bytes 1310720 | tf_op jit(solution)/shard_map/all_gather | solution.py:39
  339.0 407.4 %all-reduce.2.cloned.1.call-start = ((), (), s32[]{:S(2)}) async-start(), calls=%async_computation.6 | async-start | bytes 1966080 | tf_op jit(solution)/shard_map/psum | solution.py:139
  355.8 49.0 %collective-permute-start.4 = (bf16[1,16,256,128]{3,2,1,0:T(8,128)(2,1)}, bf16[1,16,256,128]{3,2,1,0:T(8,128)(2,1)S(1)}, u32[]{:S(2)}, u32[]{:S(2)}) collective-permute-start(bf16[1,16,256,128]{3,2,1,0:T(8,128)(2,1)} %bitcast.239), channel_id=1, source_target_pairs={{0,4},{4,8},{8,12},{12,16},{16,20},{20,24},{24,28},{1,5},{5,9},{9,... | collective-permute-start | bytes 3145736 | tf_op jit(solution)/shard_map/ppermute | solution.py:16
  359.3 45.5 %collective-permute-start.5 = (bf16[1,16,256,128]{3,2,1,0:T(8,128)(2,1)}, bf16[1,16,256,128]{3,2,1,0:T(8,128)(2,1)S(1)}, u32[]{:S(2)}, u32[]{:S(2)}) collective-permute-start(bf16[1,16,256,128]{3,2,1,0:T(8,128)(2,1)} %bitcast.240), channel_id=1, source_target_pairs={{4,0},{8,4},{12,8},{16,12},{20,16},{24,20},{28,24},{5,1},{9,5},{13... | collective-permute-start | bytes 3145736 | tf_op jit(solution)/shard_map/ppermute | solution.py:17
  427.5 3.5 copy-start.1
  432.6 3.3 copy-start.2
  449.8 3.5 copy-start.1
  455.0 3.3 copy-start.2
  472.1 3.5 copy-start.1
  477.3 3.3 copy-start.2
  494.4 3.5 copy-start.1
  499.6 3.3 copy-start.2
  516.8 3.5 copy-start.1
  521.9 3.3 copy-start.2
  525.9 11.7 %copy-start.3 = (f32[1920,128]{1,0:T(8,128)S(1)}, f32[1920,128]{1,0:T(8,128)}, u32[]{:S(2)}) copy-start(f32[1920,128]{1,0:T(8,128)} %get-tuple-element.510) | copy-start | bytes 2949124
  530.6 73.1 %collective-permute-start.6 = (f32[16,256,128]{2,1,0:T(8,128)}, f32[16,256,128]{2,1,0:T(8,128)}, u32[]{:S(2)}, u32[]{:S(2)}) collective-permute-start(f32[16,256,128]{2,1,0:T(8,128)} %get-tuple-element.657), channel_id=1, source_target_pairs={{0,4},{4,8},{8,12},{12,16},{16,20},{20,24},{24,28},{1,5},{5,9},{9,... | collective-permute-start | bytes 6291464 | tf_op jit(solution)/shard_map/ppermute | solution.py:25
  536.2 67.5 %collective-permute-start.7 = (f32[16,256,128]{2,1,0:T(8,128)}, f32[16,256,128]{2,1,0:T(8,128)}, u32[]{:S(2)}, u32[]{:S(2)}) collective-permute-start(f32[16,256,128]{2,1,0:T(8,128)} %get-tuple-element.658), channel_id=1, source_target_pairs={{4,0},{8,4},{12,8},{16,12},{20,16},{24,20},{28,24},{5,1},{9,5},{13... | collective-permute-start | bytes 6291464 | tf_op jit(solution)/shard_map/ppermute | solution.py:25
  539.8 240.4 %reduce-scatter.5.cloned.1.call-start = ((), (), s32[]{:S(2)}) async-start(), calls=%async_computation.5 | async-start | bytes 2621440 | tf_op jit(solution)/shard_map/reduce_scatter | solution.py:46
Sparse Core Ops, SparseCore 0:
  10.1 19.4 all-gather.2
  260.5 76.2 reduce-scatter.2
  339.1 16.6 all-gather.4
  539.9 206.3 all-reduce.1
  748.7 31.4 reduce-scatter.4
where the time goes:
time: 794 us; the launch traced here: 789 us
  waiting for transfers between devices  505 us (64%)
  matrix products  110 us (14%)
  loops' own time  52.6 us (7%)
  local copies, waits for them, and re-layouts  44.5 us (6%)
  other arithmetic  40.3 us (5%)
  starting transfers between devices  22.4 us (3%)
  between operations  14 us (2%)
    psum x1, waiting for transfers between devices, body(): total_weights = lax.psum(local_weights, ('block', 'grp'))  138 us
    ppermute x4, waiting for transfers between devices, shifted(): return lax.ppermute(block, axis, route)  135 us
    reduce_scatter x2, waiting for transfers between devices, collect(): lax.psum_scatter(partial_value[1] + from_lower + from_upper, 'grp', scatt...  108 us
    ppermute x2, waiting for transfers between devices, with_halo(): before = lax.ppermute(last, axis, up)  87.4 us
    all_gather x2, waiting for transfers between devices, neighbours(): region = lax.all_gather(values, 'grp', axis=0, tiled=True)  36.5 us
    another operation x1, loops' own time, body(): lax.fori_loop(0, used, forward_pair, (own_zero, sent_zero, store_zero, st...  26.9 us
    another operation x1, loops' own time, body(): lax.fori_loop(0, used, backward_pair, (own_zero, sent_zero, weight_zero,...  25.7 us
    dot_general x5, matrix products, backward_pair(): jnp.einsum('kij,ikc->jc', tile, back_near, preferred_element_type=jnp.flo...  18.1 us
  transfers between devices with their start and end apart: 13, of which 9 were waited for; matrix products, arithmetic and copies ran while one was open for 1% of the time, Pallas kernels for 0%

commit v1 on v0

v1 whole, which is shorter than its diff:
```python
import functools
import math

import jax
import jax.numpy as jnp
from jax import lax
from jax.experimental import pallas as pl
from jax.experimental.pallas import tpu as pltpu
from jax.sharding import PartitionSpec as P

MESH = pl.DeviceIdType.MESH
F32, BF16 = jnp.float32, jnp.bfloat16
VMEM_BYTES = 56 * 2**20
PARTS = 2
VMEM = pl.BlockSpec(memory_space=pltpu.VMEM)
SMEM = pl.BlockSpec(memory_space=pltpu.SMEM)


def low_bit(mask):
    return mask & -mask


def grp_masks(groups):
    return sorted(range(1, groups), key=lambda m: (-low_bit(m), m))


def grp_bits(groups):
    return [1 << i for i in reversed(range(groups.bit_length() - 1))]


def where_am_i(columns):
    b, g = lax.axis_index("block"), lax.axis_index("grp")
    return b, g, {0: b > 0, 1: None, 2: b < columns - 1}


def under(condition, action):
    if condition is None:
        action()
    else:
        pl.when(condition)(action)


def greet(columns, groups):
    b, g, has = where_am_i(columns)
    barrier = pltpu.get_barrier_semaphore()
    for bit in grp_bits(groups):
        pl.semaphore_signal(barrier, inc=1, device_id=(b, g ^ bit), device_id_type=MESH)
    for side, step in ((0, -1), (2, 1)):
        @pl.when(has[side])
        def _():
            pl.semaphore_signal(barrier, inc=1, device_id=(b + step, g), device_id_type=MESH)
    peers = len(grp_bits(groups)) + has[0].astype(jnp.int32) + has[2].astype(jnp.int32)
    pl.semaphore_wait(barrier, peers)


def spread(near, send_sem, recv_sem, columns):
    b, g, has = where_am_i(columns)
    groups, blocks = near.shape[1], near.shape[2]
    span = blocks // PARTS
    opposite = {0: 2, 2: 0}

    def at(col, mask, part):
        return near.at[col, g ^ mask, pl.ds(part * span, span)]

    def sem(col, mask, part):
        return (col * groups + mask) * PARTS + part

    def side_copy(col, part):
        i = sem(col, 0, part)
        step = 1 if col == 0 else -1
        return pltpu.make_async_remote_copy(
            src_ref=at(1, 0, part), dst_ref=at(col, 0, part), send_sem=send_sem.at[i],
            recv_sem=recv_sem.at[i], device_id=(b + step, g), device_id_type=MESH)

    def grp_copy(col, mask, part):
        bit = low_bit(mask)
        i = sem(col, mask, part)
        return pltpu.make_async_remote_copy(
            src_ref=at(col, mask ^ bit, part), dst_ref=at(col, mask ^ bit, part), send_sem=send_sem.at[i],
            recv_sem=recv_sem.at[i], device_id=(b, g ^ bit), device_id_type=MESH)

    def arrival(col, mask, part):
        bit = low_bit(mask)
        i = sem(col, mask, part)
        return pltpu.make_async_remote_copy(
            src_ref=at(col, mask ^ bit, part), dst_ref=at(col, mask, part), send_sem=send_sem.at[i],
            recv_sem=recv_sem.at[i], device_id=(b, g ^ bit), device_id_type=MESH)

    def forward(col, mask, part):
        for bit in grp_bits(groups):
            if mask == 0 or bit < low_bit(mask):
                grp_copy(col, mask | bit, part).start()

    parts = range(PARTS)
    for part in parts:
        for col in (0, 2):
            pl.when(has[opposite[col]])(lambda: side_copy(col, part).start())
        forward(1, 0, part)
    for part in parts:
        for col in (0, 2):
            @pl.when(has[col])
            def _():
                side_copy(col, part).wait_recv()
                forward(col, 0, part)
    masks = grp_masks(groups)
    for mask in masks:
        for part in parts:
            for col in (1, 0, 2):
                def step():
                    arrival(col, mask, part).wait_recv()
                    forward(col, mask, part)
                under(has[col], step)
    for part in parts:
        for col in (0, 2):
            pl.when(has[opposite[col]])(lambda: side_copy(col, part).wait_send())
    for mask in masks:
        for part in parts:
            for col in (0, 1, 2):
                under(has[col], lambda: grp_copy(col, mask, part).wait_send())


def add_blocks(out, one, two, span):
    for i in range(span):
        out[i] = (one[i].astype(F32) + two[i].astype(F32)).astype(BF16)


def gather_back(sent, acc, land, beside, send_sem, recv_sem, columns):
    b, g, has = where_am_i(columns)
    groups, blocks = sent.shape[1], sent.shape[2]
    span = blocks // PARTS
    opposite = {0: 2, 2: 0}
    cols = (0, 2, 1)
    parts = range(PARTS)
    masks = grp_masks(groups)

    def cut(part):
        return pl.ds(part * span, span)

    def sem(col, mask, part):
        return (col * groups + mask) * PARTS + part

    def grp_copy(col, mask, part):
        bit = low_bit(mask)
        i = sem(col, mask, part)
        src = sent.at[col, g ^ mask, cut(part)] if bit == 1 else acc.at[col, mask, cut(part)]
        return pltpu.make_async_remote_copy(
            src_ref=src, dst_ref=land.at[col, mask, cut(part)], send_sem=send_sem.at[i],
            recv_sem=recv_sem.at[i], device_id=(b, g ^ bit), device_id_type=MESH)

    def side_copy(col, part):
        i = sem(col, 0, part)
        step, slot = (-1, 1) if col == 0 else (1, 0)
        return pltpu.make_async_remote_copy(
            src_ref=acc.at[col, 0, cut(part)], dst_ref=beside.at[slot, cut(part)], send_sem=send_sem.at[i],
            recv_sem=recv_sem.at[i], device_id=(b + step, g), device_id_type=MESH)

    odd = [m for m in masks if m & 1]
    for mask in sorted(odd, reverse=True):
        for part in parts:
            for col in cols:
                under(has[col], lambda: grp_copy(col, mask, part).start())
    for bit in reversed(grp_bits(groups)):
        kept = [m for m in range(groups) if m % (2 * bit) == 0]
        for mask in sorted(kept, reverse=True):
            for part in parts:
                for col in cols:
                    def step():
                        grp_copy(col, mask | bit, part).wait_recv()
                        held = sent.at[col, g ^ mask, cut(part)] if bit == 1 else acc.at[col, mask, cut(part)]
                        add_blocks(acc.at[col, mask, cut(part)], held, land.at[col, mask | bit, cut(part)], span)
                        if mask and low_bit(mask) == 2 * bit:
                            grp_copy(col, mask, part).start()
                        if 2 * bit == groups and col != 1:
                            side_copy(col, part).start()
                    under(has[col], step)
    for part in parts:
        for col in (0, 2):
            pl.when(has[opposite[col]])(lambda: side_copy(col, part).wait_recv())
    for part in parts:
        for col in (0, 2):
            pl.when(has[col])(lambda: side_copy(col, part).wait_send())
        for mask in masks:
            for col in cols:
                under(has[col], lambda: grp_copy(col, mask, part).wait_send())


def reduced_rows(own, acc, beside, total, columns):
    _, _, has = where_am_i(columns)
    for i in range(total.shape[0]):
        total[i] = own[i] + acc[1, 0, i].astype(F32)
    for slot, col in ((0, 0), (1, 2)):
        @pl.when(has[col])
        def _():
            for i in range(total.shape[0]):
                total[i] += beside[slot, i].astype(F32)


def rows_below(count, shape):
    return lax.broadcasted_iota(jnp.int32, shape, 0) < count


def spread_features(columns, counts, features, near, send_sem, recv_sem):
    _, g, _ = where_am_i(columns)
    blocks = features.shape[0]
    for i in range(blocks):
        rows = features[i].astype(F32)
        near[1, g, i] = jnp.where(rows_below(counts[i], rows.shape), rows, 0.0).astype(BF16)
    greet(columns, near.shape[1])
    spread(near, send_sem, recv_sem, columns)


def finish_forward(columns, counts, own, sent, cotangent, activated, near,
                   acc, land, beside, total, send_sem, recv_sem, send_sem2, recv_sem2):
    _, g, _ = where_am_i(columns)
    greet(columns, near.shape[1])
    gather_back(sent, acc, land, beside, send_sem, recv_sem, columns)
    reduced_rows(own, acc, beside, total, columns)
    for i in range(total.shape[0]):
        keep = rows_below(counts[i], total.shape[1:])
        pre = jnp.where(keep, total[i], 0.0)
        sig = jax.nn.sigmoid(pre)
        activated[i] = (pre * sig).astype(BF16)
        slope = sig * (1.0 + pre * (1.0 - sig))
        near[1, g, i] = jnp.where(keep, cotangent[i].astype(F32) * slope, 0.0).astype(BF16)
    spread(near, send_sem2, recv_sem2, columns)


def finish_backward(columns, counts, own, sent, grad, acc, land, beside, total, send_sem, recv_sem):
    greet(columns, sent.shape[1])
    gather_back(sent, acc, land, beside, send_sem, recv_sem, columns)
    reduced_rows(own, acc, beside, total, columns)
    for i in range(total.shape[0]):
        keep = rows_below(counts[i], total.shape[1:])
        grad[i] = jnp.where(keep, total[i], 0.0).astype(BF16)


def dot(a, b):
    return jnp.dot(a, b, preferred_element_type=F32)


def zero_blocks(ref):
    def clear(i, carry):
        ref[i] = jnp.zeros(ref.shape[1:], ref.dtype)
        return carry
    lax.fori_loop(0, ref.shape[0], clear, 0)


def forward_slots(first_of, near_of, base, used, tile, near, weights, mirror_t, own, sent, left, right):
    slot = pl.program_id(0)
    kernels, width = tile.shape[1], near.shape[2]

    @pl.when(slot == 0)
    def _():
        zero_blocks(own)
        zero_blocks(sent)

    @pl.when(slot < used[0])
    def _():
        first, second = first_of[slot], near_of[slot]
        right[...] = dot(near[second], weights[...]).astype(BF16)
        rows_t = near[base[0] + first].astype(F32).T.astype(BF16)
        left[...] = dot(mirror_t[...], rows_t).astype(BF16)
        to_first = jnp.zeros(own.shape[1:], F32)
        to_second = jnp.zeros(own.shape[1:][::-1], F32)
        for k in range(kernels):
            cut = pl.ds(k * width, width)
            to_first += dot(tile[0, k], right[:, cut])
            to_second += dot(left[cut, :], tile[0, k])
        own[first] += to_first
        sent[second] = (sent[second].astype(F32) + to_second.T).astype(BF16)


def backward_slots(first_of, near_of, base, used, tile, near, near_up, weights, mirror_t,
                   own, sent, grad_near, grad_own, up_t, up_own):
    slot = pl.program_id(0)
    kernels, width = tile.shape[1], near.shape[2]

    @pl.when(slot == 0)
    def _():
        zero_blocks(own)
        zero_blocks(sent)
        grad_near[...] = jnp.zeros_like(grad_near)
        grad_own[...] = jnp.zeros_like(grad_own)

    @pl.when(slot < used[0])
    def _():
        first, second = first_of[slot], near_of[slot]
        up_first_t = near_up[base[0] + first].astype(F32).T.astype(BF16)
        up_second = near_up[second]
        for k in range(kernels):
            cut = pl.ds(k * width, width)
            up_t[cut, :] = dot(up_first_t, tile[0, k]).astype(BF16)
            up_own[:, cut] = dot(tile[0, k], up_second).astype(BF16)
        rows_t = near[base[0] + first].astype(F32).T.astype(BF16)
        grad_near[...] += dot(up_t[...], near[second])
        grad_own[...] += dot(rows_t, up_own[...])
        to_second = dot(weights[...], up_t[...])
        own[first] += dot(up_own[...], mirror_t[...])
        sent[second] = (sent[second].astype(F32) + to_second.T).astype(BF16)


def body(features, point_counts, kernel_weights, influence, pair_list, pair_counts, cotangent):
    blocks, points, width = features.shape
    kernels = kernel_weights.shape[0]
    slots = influence.shape[0]
    columns, groups = lax.axis_size("block"), lax.axis_size("grp")
    b, g = lax.axis_index("block"), lax.axis_index("grp")
    region = groups * blocks
    flat = (3 * region, points, width)
    spread_shape = (3, groups, blocks, points, width)
    own_shape = (blocks, points, width)
    copies = 3 * groups * PARTS

    used = pair_counts
    first_of = pair_list[:, 0]
    near_of = pair_list[:, 1] - (b - 1) * region
    base = (region + g * blocks).astype(jnp.int32)[None]
    weights = kernel_weights.transpose(1, 0, 2).reshape(width, kernels * width)
    mirror_t = kernel_weights[::-1].transpose(0, 2, 1).reshape(kernels * width, width)

    def remote(kernel, collective, ins, outs, scratch, args):
        return pl.pallas_call(
            functools.partial(kernel, columns),
            in_specs=ins,
            out_specs=[VMEM] * len(outs),
            out_shape=outs,
            scratch_shapes=scratch,
            compiler_params=pltpu.CompilerParams(
                collective_id=collective, has_side_effects=True, vmem_limit_bytes=VMEM_BYTES),
        )(*args)

    dma = pltpu.SemaphoreType.DMA((copies,))
    reduce_scratch = [
        pltpu.VMEM(spread_shape, BF16), pltpu.VMEM(spread_shape, BF16),
        pltpu.VMEM((2, *own_shape), BF16), pltpu.VMEM(own_shape, F32), dma, dma]
    near_type = jax.ShapeDtypeStruct(spread_shape, BF16)
    own_type = jax.ShapeDtypeStruct(own_shape, BF16)

    def tile_at(slot, first_of, near_of, base, used):
        return (jnp.minimum(slot, used[0] - 1), 0, 0, 0)

    def fixed(shape):
        return pl.BlockSpec(shape, lambda slot, *_: (0,) * len(shape))

    def local(kernel, ins, outs, scratch, args):
        return pl.pallas_call(
            kernel,
            grid_spec=pltpu.PrefetchScalarGridSpec(
                num_scalar_prefetch=4, grid=(slots,),
                in_specs=[pl.BlockSpec((1, kernels, points, points), tile_at)] + [fixed(a.shape) for a in ins],
                out_specs=[fixed(a.shape) for a in outs],
                scratch_shapes=scratch),
            out_shape=outs,
            compiler_params=pltpu.CompilerParams(vmem_limit_bytes=VMEM_BYTES),
        )(first_of, near_of, base, used, influence, *args)

    (near,) = remote(spread_features, 0, [SMEM, VMEM], [near_type], [dma, dma], (point_counts, features))
    near_rows = near.reshape(flat)
    slot_outs = [jax.ShapeDtypeStruct(own_shape, F32), jax.ShapeDtypeStruct(flat, BF16)]
    ins = (near_rows, weights, mirror_t)
    own, sent = local(
        forward_slots, ins, slot_outs,
        [pltpu.VMEM((kernels * width, points), BF16), pltpu.VMEM((points, kernels * width), BF16)], ins)
    activated, near_up = remote(
        finish_forward, 1, [SMEM, VMEM, VMEM, VMEM], [own_type, near_type],
        reduce_scratch + [dma, dma],
        (point_counts, own, sent.reshape(spread_shape), cotangent))
    ins = (near_rows, near_up.reshape(flat), weights, mirror_t)
    own, sent, grad_near, grad_own = local(
        backward_slots, ins,
        slot_outs + [jax.ShapeDtypeStruct((kernels * width, width), F32),
                     jax.ShapeDtypeStruct((width, kernels * width), F32)],
        [pltpu.VMEM((kernels * width, points), BF16), pltpu.VMEM((points, kernels * width), BF16)], ins)
    local_weights = (
        grad_near.reshape(kernels, width, width).transpose(0, 2, 1)
        + grad_own.reshape(width, kernels, width).transpose(1, 0, 2)[::-1])
    total_weights = lax.psum(local_weights, ("block", "grp"))
    (grad_features,) = remote(
        finish_backward, 2, [SMEM, VMEM, VMEM], [own_type], reduce_scratch,
        (point_counts, own, sent.reshape(spread_shape)))
    total_points = blocks * points * columns * groups
    grad_weights = total_weights * (1.0 / math.sqrt(total_points))
    return (activated, grad_features, grad_weights)


def solution(mesh):
    placed = (
        P(("block", "grp"), None, None),
        P(("block", "grp")),
        P(),
        P(("block", "grp"), None, None, None),
        P(("block", "grp"), None),
        P(("block", "grp")),
        P(("block", "grp"), None, None),
    )
    return jax.shard_map(
        body,
        mesh=mesh,
        in_specs=placed,
        out_specs=(P(("block", "grp"), None, None), P(("block", "grp"), None, None), P()),
        check_vma=False,
    )
```

time: 794 us -> 273 us (0.34)
  waiting for transfers between devices: 505 us -> 104 us
  Pallas kernels: 0 us -> 142 us
  matrix products: 110 us -> 0 us
  loops' own time: 52.6 us -> 0 us
  other arithmetic: 40.3 us -> 4.06 us
  local copies, waits for them, and re-layouts: 44.5 us -> 8.59 us
  starting transfers between devices: 22.4 us -> 0.04 us
    ppermute x8 -> x0, waiting for transfers between devices: 222 us -> none  [the longest x4 135 us: shifted(): return lax.ppermute(block, axis, route)]
    pallas_call x0 -> x5, Pallas kernels: none -> 142 us  [the longest x3 118 us: remote(): pl.pallas_call(functools.partial(kernel, columns), in_specs=ins, out_spec...]
    dot_general x50 -> x0, matrix products: 110 us -> none  [the longest x5 18.1 us: backward_pair(): jnp.einsum('kij,ikc->jc', tile, back_near, preferred_element_type=jnp.flo...]
    reduce_scatter x2 -> x0, waiting for transfers between devices: 108 us -> none  [collect(): lax.psum_scatter(partial_value[1] + from_lower + from_upper, 'grp', scatt...]
    another operation x2 -> x0, loops' own time: 52.6 us -> none  [the longest x1 26.9 us: body(): lax.fori_loop(0, used, forward_pair, (own_zero, sent_zero, store_zero, st...]
    all_gather x2 -> x0, waiting for transfers between devices: 36.5 us -> none  [neighbours(): region = lax.all_gather(values, 'grp', axis=0, tiled=True)]
    psum x1, waiting for transfers between devices: 138 us -> 104 us  [body(): total_weights = lax.psum(local_weights, ('block', 'grp'))]
    ppermute x8 -> x0, starting transfers between devices: 22.2 us -> none  [the longest x4 12.7 us: shifted(): return lax.ppermute(block, axis, route)]
  transfers between devices with their start and end apart: 13 -> 1, of which waited for: 9 -> 1; matrix products, arithmetic and copies ran while one was open for 1% -> 0% of each run, Pallas kernels for 0% -> 15%
where the time goes in v1:
time: 273 us
  Pallas kernels  142 us (52%)
  waiting for transfers between devices  104 us (38%)
  between operations  14.8 us (5%)
  local copies, waits for them, and re-layouts  8.59 us (3%)
  other arithmetic  4.06 us (1%)
    pallas_call x3, Pallas kernels, remote(): pl.pallas_call(functools.partial(kernel, columns), in_specs=ins, out_spec...  118 us
    psum x1, waiting for transfers between devices, body(): total_weights = lax.psum(local_weights, ('block', 'grp'))  104 us
    pallas_call x2, Pallas kernels, local(): pl.pallas_call(kernel, grid_spec=pltpu.PrefetchScalarGridSpec(num_scalar_...  23.8 us
  transfers between devices with their start and end apart: 1, of which 1 were waited for; matrix products, arithmetic and copies ran while one was open for 0% of the time, Pallas kernels for 15%

profile of v1, /device:TPU:0, one launch (start us, length us, event | category | flops | bytes accessed | tf_op | source)
XLA Modules:
  0.0 273.2 jit_solution(8575257700769971961)
XLA Ops:
  7.2 0.0 copy-start.2
  7.2 0.0 all-reduce.2.cloned.1.call-start
  7.2 1.1 reverse_bitcast_fusion
  8.3 1.3 copy.14
  10.3 1.0 copy.15
  11.2 1.0 copy.16.weights
  12.2 0.0 copy-done.2
  12.3 0.5 subtract_bitcast_fusion
  12.8 20.2 %shard_map.94 = bf16[3,4,4,256,128]{4,3,2,1,0:T(8,128)(2,1)} custom-call(s32[4]{0:T(128)} %counts.5, bf16[4,256,128]{2,1,0:T(8,128)(2,1)} %features.1), custom_call_target="tpu_custom_call" | custom-call | tf_op jit(solution)/shard_map/pallas_call | solution.py:322
  33.0 10.8 %shard_map.95 = (f32[4,256,128]{2,1,0:T(8,128)}, bf16[48,256,128]{2,1,0:T(8,128)(2,1)}) custom-call(s32[8]{0:T(128)} %get-tuple-element.23.first_of, s32[8]{0:T(128)} %get-tuple-element.22.near_of, s32[1]{0:T(128)} %bitcast.2.base, s32[1]{0:T(128)S(6)} %copy.23.used, bf16[8,15,256,256]{3,2,1,0:T(8,128)(2,1)} %tile.3, bf16[48,256,128]{2,1,0:T(8,128)(2,1)} %bitcast.21, ...), custom_call_target="tpu_custom_call" | custom-call | tf_op jit(solution)/shard_map/pallas_call | solution.py:346
  43.8 56.3 %shard_map.96 = (bf16[4,256,128]{2,1,0:T(8,128)(2,1)}, bf16[3,4,4,256,128]{4,3,2,1,0:T(8,128)(2,1)}) custom-call(s32[4]{0:T(128)} %counts.5, f32[4,256,128]{2,1,0:T(8,128)} %get-tuple-element.11.own, bf16[3,4,4,256,128]{4,3,2,1,0:T(8,128)(2,1)} %bitcast.27, bf16[4,256,128]{2,1,0:T(8,128)(2,1)} %cotangent.1), custom_call_target="tpu_custom_call" | custom-call | tf_op jit(solution)/shard_map/pallas_call | solution.py:322
  100.1 12.9 %shard_map.97 = (f32[4,256,128]{2,1,0:T(8,128)}, bf16[48,256,128]{2,1,0:T(8,128)(2,1)}, f32[1920,128]{1,0:T(8,128)}, f32[128,1920]{1,0:T(8,128)}) custom-call(s32[8]{0:T(128)} %get-tuple-element.23.first_of, s32[8]{0:T(128)} %get-tuple-element.22.near_of, s32[1]{0:T(128)} %bitcast.2.base, s32[1]{0:T(128)S(6)} %copy.23.used, bf16[8,15,256,256]{3,2,1,0:T(8,128)(2,1)} %tile.3, ...), custom_call_target="tpu_custom_call" | custom-call | tf_op jit(solution)/shard_map/pallas_call | solution.py:346
  113.1 1.5 copy.18
  114.6 2.3 reverse_add_fusion
  116.9 0.0 all-reduce.2.cloned.1.call-update
  116.9 0.0 copy-start.1
  116.9 41.3 %shard_map.98 = bf16[4,256,128]{2,1,0:T(8,128)(2,1)} custom-call(s32[4]{0:T(128)} %counts.5, f32[4,256,128]{2,1,0:T(8,128)} %get-tuple-element.15.own, bf16[3,4,4,256,128]{4,3,2,1,0:T(8,128)(2,1)} %bitcast.26), custom_call_target="tpu_custom_call" | custom-call | tf_op jit(solution)/shard_map/pallas_call | solution.py:322
  158.2 0.0 copy-start
  158.3 104.1 %all-reduce.2.cloned.1.call-done = f32[15,128,128]{1,2,0:T(8,128)} async-done(((f32[15,128,128]{1,2,0:T(8,128)}), f32[15,128,128]{1,2,0:T(8,128)}) %all-reduce.2.cloned.1.call-update) | async-done | bytes 983056 | tf_op jit(solution)/shard_map/psum | solution.py:377
  262.4 1.3 broadcast_multiply_fusion
  263.7 1.3 copy.19
  265.0 0.0 copy-done.1
  265.0 0.7 copy.24
  265.7 0.0 copy-done
  265.7 0.7 copy.25
Async XLA Ops:
  7.2 5.1 %copy-start.2 = (s32[8,2]{0,1:T(2,128)S(1)}, s32[8,2]{0,1:T(2,128)}, u32[]{:S(2)}) copy-start(s32[8,2]{0,1:T(2,128)} %param.11) | copy-start | bytes 196
  7.2 255.2 %all-reduce.2.cloned.1.call-start = ((), (), s32[]{:S(2)}) async-start(), calls=%async_computation | async-start | bytes 1966080 | tf_op jit(solution)/shard_map/psum | solution.py:377
  116.9 148.1 %copy-start.1 = (bf16[4,256,128]{2,1,0:T(8,128)(2,1)S(1)}, bf16[4,256,128]{2,1,0:T(8,128)(2,1)}, u32[]{:S(2)}) copy-start(bf16[4,256,128]{2,1,0:T(8,128)(2,1)} %get-tuple-element.27) | copy-start | bytes 786436
  158.2 107.4 %copy-start = (bf16[4,256,128]{2,1,0:T(8,128)(2,1)S(1)}, bf16[4,256,128]{2,1,0:T(8,128)(2,1)}, u32[]{:S(2)}) copy-start(bf16[4,256,128]{2,1,0:T(8,128)(2,1)} %shard_map.98) | copy-start | bytes 786436
Sparse Core Ops, SparseCore 0:
  117.0 145.3 all-reduce.1

commit v2 on v1

--- a/solution.py
+++ b/solution.py
@@ -11,7 +11,7 @@
 MESH = pl.DeviceIdType.MESH
 F32, BF16 = jnp.float32, jnp.bfloat16
 VMEM_BYTES = 56 * 2**20
-PARTS = 2
+PARTS = 4
 VMEM = pl.BlockSpec(memory_space=pltpu.VMEM)
 SMEM = pl.BlockSpec(memory_space=pltpu.SMEM)
 
@@ -40,16 +40,23 @@
         pl.when(condition)(action)
 
 
-def greet(columns, groups):
+def greet(columns, groups, whole_axis=False):
     b, g, has = where_am_i(columns)
     barrier = pltpu.get_barrier_semaphore()
+    peers = len(grp_bits(groups))
     for bit in grp_bits(groups):
         pl.semaphore_signal(barrier, inc=1, device_id=(b, g ^ bit), device_id_type=MESH)
-    for side, step in ((0, -1), (2, 1)):
-        @pl.when(has[side])
-        def _():
-            pl.semaphore_signal(barrier, inc=1, device_id=(b + step, g), device_id_type=MESH)
-    peers = len(grp_bits(groups)) + has[0].astype(jnp.int32) + has[2].astype(jnp.int32)
+    if whole_axis:
+        for distance in range(1, columns):
+            pl.semaphore_signal(
+                barrier, inc=1, device_id=(lax.rem(b + distance, columns), g), device_id_type=MESH)
+        peers = peers + columns - 1
+    else:
+        for side, step in ((0, -1), (2, 1)):
+            @pl.when(has[side])
+            def _():
+                pl.semaphore_signal(barrier, inc=1, device_id=(b + step, g), device_id_type=MESH)
+        peers = peers + has[0].astype(jnp.int32) + has[2].astype(jnp.int32)
     pl.semaphore_wait(barrier, peers)
 
 
@@ -119,6 +126,14 @@
                 under(has[col], lambda: grp_copy(col, mask, part).wait_send())
 
 
+def run(*steps):
+    for _ in zip(*steps):
+        pass
+    for step in steps:
+        for _ in step:
+            pass
+
+
 def add_blocks(out, one, two, span):
     for i in range(span):
         out[i] = (one[i].astype(F32) + two[i].astype(F32)).astype(BF16)
@@ -159,6 +174,7 @@
         for part in parts:
             for col in cols:
                 under(has[col], lambda: grp_copy(col, mask, part).start())
+    yield
     for bit in reversed(grp_bits(groups)):
         kept = [m for m in range(groups) if m % (2 * bit) == 0]
         for mask in sorted(kept, reverse=True):
@@ -173,6 +189,9 @@
                         if 2 * bit == groups and col != 1:
                             side_copy(col, part).start()
                     under(has[col], step)
+                if 2 * bit == groups and part == PARTS // 2 - 1:
+                    yield
+            yield
     for part in parts:
         for col in (0, 2):
             pl.when(has[opposite[col]])(lambda: side_copy(col, part).wait_recv())
@@ -213,7 +232,7 @@
                    acc, land, beside, total, send_sem, recv_sem, send_sem2, recv_sem2):
     _, g, _ = where_am_i(columns)
     greet(columns, near.shape[1])
-    gather_back(sent, acc, land, beside, send_sem, recv_sem, columns)
+    run(gather_back(sent, acc, land, beside, send_sem, recv_sem, columns))
     reduced_rows(own, acc, beside, total, columns)
     for i in range(total.shape[0]):
         keep = rows_below(counts[i], total.shape[1:])
@@ -225,9 +244,100 @@
     spread(near, send_sem2, recv_sem2, columns)
 
 
-def finish_backward(columns, counts, own, sent, grad, acc, land, beside, total, send_sem, recv_sem):
-    greet(columns, sent.shape[1])
-    gather_back(sent, acc, land, beside, send_sem, recv_sem, columns)
+def sum_weights(scale, terms, out, land, held, low, low_land, mixed, gathered, send_sem, recv_sem, columns):
+    b, g, _ = where_am_i(columns)
+    groups = terms.shape[0]
+    bits = grp_bits(groups)
+    base_a, base_b, base_c = groups, groups + columns, groups + 2 * columns
+    distances = range(1, columns)
+
+    def copy(src, dst, i, device):
+        return pltpu.make_async_remote_copy(
+            src_ref=src, dst_ref=dst, send_sem=send_sem.at[i], recv_sem=recv_sem.at[i],
+            device_id=device, device_id_type=MESH)
+
+    def halve(mask):
+        bit = low_bit(mask)
+        if bit == 1:
+            return copy(terms.at[g ^ mask], land.at[mask], mask, (b, g ^ bit))
+        return copy(low.at[mask], low_land.at[mask], mask, (b, g ^ bit))
+
+    def share(distance):
+        peer = lax.rem(b + distance, columns)
+        return copy(low.at[0, peer], mixed.at[distance], base_a + distance, (peer, g))
+
+    def tell(distance):
+        peer = lax.rem(b + distance, columns)
+        return copy(gathered.at[g, b], gathered.at[g, b], base_b + distance, (peer, g))
+
+    def told(distance):
+        peer = lax.rem(b + columns - distance, columns)
+        return copy(gathered.at[g, b], gathered.at[g, peer], base_b + distance, (peer, g))
+
+    def double(mask):
+        piece = gathered.at[g ^ mask ^ low_bit(mask)]
+        return copy(piece, piece, base_c + mask, (b, g ^ low_bit(mask)))
+
+    def doubled(mask):
+        return copy(gathered.at[g], gathered.at[g ^ mask], base_c + mask, (b, g ^ low_bit(mask)))
+
+    masks = grp_masks(groups)
+    for mask in masks:
+        if mask & 1:
+            halve(mask).start()
+    yield
+    for bit in reversed(bits):
+        for mask in sorted((m for m in range(groups) if m % (2 * bit) == 0), reverse=True):
+            halve(mask | bit).wait_recv()
+            for n in range(columns):
+                if bit == 1:
+                    value = terms[g ^ mask, n] + land[mask | 1, n]
+                else:
+                    value = held[mask, n] + low_land[mask | bit, n].astype(F32)
+                held[mask, n] = value
+                low[mask, n] = value.astype(BF16)
+            if mask and low_bit(mask) == 2 * bit:
+                halve(mask).start()
+        if 2 * bit == groups:
+            for distance in distances:
+                share(distance).start()
+        yield
+    for distance in distances:
+        share(distance).wait_recv()
+    total = held[0, b]
+    for distance in distances:
+        total += mixed[distance].astype(F32)
+    gathered[g, b] = total.astype(BF16)
+    for distance in distances:
+        tell(distance).start()
+    yield
+    for distance in distances:
+        told(distance).wait_recv()
+    for bit in bits:
+        double(bit).start()
+    yield
+    for mask in masks:
+        doubled(mask).wait_recv()
+        for bit in bits:
+            if bit < low_bit(mask):
+                double(mask | bit).start()
+        if low_bit(mask) == 2:
+            yield
+    for mask in masks:
+        halve(mask).wait_send()
+        double(mask).wait_send()
+    for distance in distances:
+        share(distance).wait_send()
+        tell(distance).wait_send()
+    for h in range(groups):
+        out[h] = gathered[h].astype(F32) * scale
+
+
+def finish_backward(scale, columns, counts, own, sent, terms, grad, summed, acc, land, beside, total, send_sem, recv_sem,
+                    w_land, w_held, w_low, w_low_land, w_mixed, w_gathered, w_send, w_recv):
+    greet(columns, sent.shape[1], True)
+    run(sum_weights(scale, terms, summed, w_land, w_held, w_low, w_low_land, w_mixed, w_gathered, w_send, w_recv, columns),
+        gather_back(sent, acc, land, beside, send_sem, recv_sem, columns))
     reduced_rows(own, acc, beside, total, columns)
     for i in range(total.shape[0]):
         keep = rows_below(counts[i], total.shape[1:])
@@ -271,7 +381,7 @@
 
 
 def backward_slots(first_of, near_of, base, used, tile, near, near_up, weights, mirror_t,
-                   own, sent, grad_near, grad_own, up_t, up_own):
+                   own, sent, grads, grad_near, grad_own, up_t, up_own):
     slot = pl.program_id(0)
     kernels, width = tile.shape[1], near.shape[2]
 
@@ -298,6 +408,14 @@
         own[first] += dot(up_own[...], mirror_t[...])
         sent[second] = (sent[second].astype(F32) + to_second.T).astype(BF16)
 
+    @pl.when(slot == pl.num_programs(0) - 1)
+    def _():
+        for k in range(kernels):
+            mirrored = kernels - 1 - k
+            grads[k] = grad_near[k * width:(k + 1) * width, :].T + grad_own[:, mirrored * width:(mirrored + 1) * width]
+        for k in range(kernels, grads.shape[0]):
+            grads[k] = jnp.zeros(grads.shape[1:], F32)
+
 
 def body(features, point_counts, kernel_weights, influence, pair_list, pair_counts, cotangent):
     blocks, points, width = features.shape
@@ -366,20 +484,23 @@
         reduce_scratch + [dma, dma],
         (point_counts, own, sent.reshape(spread_shape), cotangent))
     ins = (near_rows, near_up.reshape(flat), weights, mirror_t)
-    own, sent, grad_near, grad_own = local(
-        backward_slots, ins,
-        slot_outs + [jax.ShapeDtypeStruct((kernels * width, width), F32),
-                     jax.ShapeDtypeStruct((width, kernels * width), F32)],
-        [pltpu.VMEM((kernels * width, points), BF16), pltpu.VMEM((points, kernels * width), BF16)], ins)
-    local_weights = (
-        grad_near.reshape(kernels, width, width).transpose(0, 2, 1)
-        + grad_own.reshape(width, kernels, width).transpose(1, 0, 2)[::-1])
-    total_weights = lax.psum(local_weights, ("block", "grp"))
-    (grad_features,) = remote(
-        finish_backward, 2, [SMEM, VMEM, VMEM], [own_type], reduce_scratch,
-        (point_counts, own, sent.reshape(spread_shape)))
-    total_points = blocks * points * columns * groups
-    grad_weights = total_weights * (1.0 / math.sqrt(total_points))
+    share = 16 * columns * groups
+    padded = -(-kernels * width // share) * share // width
+    own, sent, grads = local(
+        backward_slots, ins, slot_outs + [jax.ShapeDtypeStruct((padded, width, width), F32)],
+        [pltpu.VMEM((kernels * width, width), F32), pltpu.VMEM((width, kernels * width), F32),
+         pltpu.VMEM((kernels * width, points), BF16), pltpu.VMEM((points, kernels * width), BF16)], ins)
+    scale = 1.0 / math.sqrt(blocks * points * columns * groups)
+    cut = (groups, columns, padded * width // (groups * columns), width)
+    w_dma = pltpu.SemaphoreType.DMA((2 * groups + 2 * columns,))
+    grad_features, summed = remote(
+        functools.partial(finish_backward, scale), 2, [SMEM, VMEM, VMEM, VMEM],
+        [own_type, jax.ShapeDtypeStruct(cut, F32)],
+        reduce_scratch + [
+            pltpu.VMEM(cut, F32), pltpu.VMEM(cut, F32), pltpu.VMEM(cut, BF16), pltpu.VMEM(cut, BF16),
+            pltpu.VMEM(cut[1:], BF16), pltpu.VMEM(cut, BF16), w_dma, w_dma],
+        (point_counts, own, sent.reshape(spread_shape), grads.reshape(cut)))
+    grad_weights = summed.reshape(padded, width, width)[:kernels]
     return (activated, grad_features, grad_weights)
 
 

time: 273 us -> 161 us (0.59)
  waiting for transfers between devices: 104 us -> 0 us
  between operations: 14.8 us -> 1.32 us
  Pallas kernels: 142 us -> 149 us
  other arithmetic: 4.06 us -> 1.27 us
    psum x1 -> x0, waiting for transfers between devices: 104 us -> none  [body(): total_weights = lax.psum(local_weights, ('block', 'grp'))]
    pallas_call x3, Pallas kernels: 118 us -> 125 us  [remote(): pl.pallas_call(functools.partial(kernel, columns), in_specs=ins, out_spec...]
  transfers between devices with their start and end apart: 1 -> 0, of which waited for: 1 -> 0; matrix products, arithmetic and copies ran while one was open for 0% -> 0% of each run, Pallas kernels for 15% -> 0%
where the time goes in v2:
time: 161 us; the launch traced here: 160 us
  Pallas kernels  149 us (93%)
  local copies, waits for them, and re-layouts  8.99 us (6%)
    pallas_call x3, Pallas kernels, remote(): pl.pallas_call(functools.partial(kernel, columns), in_specs=ins, out_spec...  125 us
    pallas_call x2, Pallas kernels, local(): pl.pallas_call(kernel, grid_spec=pltpu.PrefetchScalarGridSpec(num_scalar_...  23.8 us
    unnamed x5, local copies, waits for them, and re-layouts  3.67 us

profile of v2, /device:TPU:0, one launch (start us, length us, event | category | flops | bytes accessed | tf_op | source)
XLA Modules:
  0.0 160.4 jit_solution(16953453711743662589)
XLA Ops:
  1.3 1.3 subtract_bitcast_fusion
  2.6 1.1 reverse_bitcast_fusion
  3.6 1.0 copy.13
  4.6 1.3 copy.12
  5.9 1.0 copy.14.weights
  6.9 20.6 %shard_map.94 = bf16[3,4,4,256,128]{4,3,2,1,0:T(8,128)(2,1)} custom-call(s32[4]{0:T(128)} %counts.5, bf16[4,256,128]{2,1,0:T(8,128)(2,1)} %features.1), custom_call_target="tpu_custom_call" | custom-call | tf_op jit(solution)/shard_map/pallas_call | solution.py:440
  27.5 10.8 %shard_map.95 = (f32[4,256,128]{2,1,0:T(8,128)}, bf16[48,256,128]{2,1,0:T(8,128)(2,1)}) custom-call(s32[8]{0:T(128)} %get-tuple-element.22.first_of, s32[8]{0:T(128)} %get-tuple-element.21.near_of, s32[1]{0:T(128)} %bitcast.2.base, s32[1]{0:T(128)S(6)} %copy.18.used, bf16[8,15,256,256]{3,2,1,0:T(8,128)(2,1)} %tile.3, bf16[48,256,128]{2,1,0:T(8,128)(2,1)} %bitcast.17, ...), custom_call_target="tpu_custom_call" | custom-call | tf_op jit(solution)/shard_map/pallas_call | solution.py:464
  38.3 56.6 %shard_map.96 = (bf16[4,256,128]{2,1,0:T(8,128)(2,1)}, bf16[3,4,4,256,128]{4,3,2,1,0:T(8,128)(2,1)}) custom-call(s32[4]{0:T(128)} %counts.5, f32[4,256,128]{2,1,0:T(8,128)} %get-tuple-element.12.own, bf16[3,4,4,256,128]{4,3,2,1,0:T(8,128)(2,1)} %bitcast.22, bf16[4,256,128]{2,1,0:T(8,128)(2,1)} %cotangent.1), custom_call_target="tpu_custom_call" | custom-call | tf_op jit(solution)/shard_map/pallas_call | solution.py:440
  94.9 13.0 %shard_map.97 = (f32[4,256,128]{2,1,0:T(8,128)}, bf16[48,256,128]{2,1,0:T(8,128)(2,1)}, f32[16,128,128]{2,1,0:T(8,128)}) custom-call(s32[8]{0:T(128)} %get-tuple-element.22.first_of, s32[8]{0:T(128)} %get-tuple-element.21.near_of, s32[1]{0:T(128)} %bitcast.2.base, s32[1]{0:T(128)S(6)} %copy.18.used, bf16[8,15,256,256]{3,2,1,0:T(8,128)(2,1)} %tile.3, ...), custom_call_target="tpu_custom_call" | custom-call | tf_op jit(solution)/shard_map/pallas_call | solution.py:464
  107.9 0.0 copy-start
  107.9 47.9 %shard_map.98 = (bf16[4,256,128]{2,1,0:T(8,128)(2,1)}, f32[4,8,64,128]{3,2,1,0:T(8,128)}) custom-call(s32[4]{0:T(128)} %counts.5, f32[4,256,128]{2,1,0:T(8,128)} %get-tuple-element.16.own, bf16[3,4,4,256,128]{4,3,2,1,0:T(8,128)(2,1)} %bitcast.21, f32[4,8,64,128]{3,2,1,0:T(8,128)} %bitcast.25), custom_call_target="tpu_custom_call" | custom-call | tf_op jit(solution)/shard_map/pallas_call | solution.py:440
  155.8 2.2 %slice.12 = f32[15,128,128]{2,1,0:T(8,128)} slice(f32[16,128,128]{2,1,0:T(8,128)} %bitcast.26), slice={[0:15], [0:128], [0:128]} | slice | bytes 1966080 | tf_op jit(solution)/shard_map/slice | solution.py:503
  158.0 0.0 copy-done
  158.0 0.7 copy.19
  158.7 1.7 %copy.20 = bf16[4,256,128]{2,1,0:T(8,128)(2,1)} copy(bf16[4,256,128]{2,1,0:T(8,128)(2,1)} %get-tuple-element.27) | data formatting | bytes 524288
Async XLA Ops:
  107.9 50.1 %copy-start = (bf16[4,256,128]{2,1,0:T(8,128)(2,1)S(1)}, bf16[4,256,128]{2,1,0:T(8,128)(2,1)}, u32[]{:S(2)}) copy-start(bf16[4,256,128]{2,1,0:T(8,128)(2,1)} %get-tuple-element.26) | copy-start | bytes 786436

commit v3 on v2

--- a/solution.py
+++ b/solution.py
@@ -103,12 +103,14 @@
         for col in (0, 2):
             pl.when(has[opposite[col]])(lambda: side_copy(col, part).start())
         forward(1, 0, part)
+    yield
     for part in parts:
         for col in (0, 2):
             @pl.when(has[col])
             def _():
                 side_copy(col, part).wait_recv()
                 forward(col, 0, part)
+    yield
     masks = grp_masks(groups)
     for mask in masks:
         for part in parts:
@@ -203,10 +205,92 @@
                 under(has[col], lambda: grp_copy(col, mask, part).wait_send())
 
 
-def reduced_rows(own, acc, beside, total, columns):
+def dot(a, b):
+    return jnp.dot(a, b, preferred_element_type=F32)
+
+
+def clear_edges(near, columns):
+    _, _, has = where_am_i(columns)
+    for col in (0, 2):
+        @pl.when(jnp.logical_not(has[col]))
+        def _():
+            def clear(h, carry):
+                for x in range(near.shape[2]):
+                    near[col, h, x] = jnp.zeros(near.shape[3:], near.dtype)
+                return carry
+            lax.fori_loop(0, near.shape[1], clear, 0)
+
+
+class Tables:
+    def __init__(self, ref, slots, blocks):
+        self.ref, self.slots, self.blocks = ref, slots, blocks
+
+    def entry(self, row, slot):
+        return self.ref[row * self.slots + slot]
+
+    def first(self, slot):
+        return self.entry(0, slot)
+
+    def second(self, slot):
+        return self.entry(1, slot), self.entry(2, slot), self.entry(3, slot)
+
+    def flag(self, slot):
+        return self.entry(4, slot).astype(F32)
+
+    def before_first(self, slot):
+        return self.entry(5, slot)
+
+    def before_second(self, slot):
+        return self.entry(6, slot)
+
+    def last_first(self, block):
+        return self.ref[7 * self.slots + block]
+
+    def last_second(self, place):
+        return self.ref[7 * self.slots + self.blocks + place]
+
+
+def table_of(pair_list, used, column, blocks, groups):
+    slots = pair_list.shape[0]
+    index = jnp.arange(slots, dtype=jnp.int32)
+    active = index < used
+    first = pair_list[:, 0]
+    owner = pair_list[:, 1] // blocks
+    col, h, x = owner // groups - column + 1, owner % groups, pair_list[:, 1] % blocks
+    place = (col * groups + h) * blocks + x
+
+    def latest(match):
+        return jnp.max(jnp.where(match, index[None, :], -1), axis=1)
+
+    def chain(key, keys):
+        earlier = (key[:, None] == key[None, :]) & active[None, :] & (index[None, :] < index[:, None])
+        found = latest(earlier)
+        here = latest((jnp.arange(keys, dtype=jnp.int32)[:, None] == key[None, :]) & active[None, :])
+        return jnp.where(found < 0, slots, found), jnp.where(here < 0, slots, here)
+
+    before_first, last_first = chain(first, blocks)
+    before_second, last_second = chain(place, 3 * groups * blocks)
+    return jnp.concatenate([first, col, h, x, active.astype(jnp.int32), before_first, before_second, last_first, last_second])
+
+
+def fetch(influence, tiles, tile_sem, slot):
+    return pltpu.make_async_copy(influence.at[slot], tiles.at[slot], tile_sem.at[slot])
+
+
+def fill_sent(sent, tables, message):
+    groups, blocks = sent.shape[1], sent.shape[2]
+    for col in range(3):
+        def place(h, carry):
+            for x in range(blocks):
+                sent[col, h, x] = message[tables.last_second((col * groups + h) * blocks + x)].astype(BF16)
+            return carry
+        lax.fori_loop(0, groups, place, 0)
+
+
+def reduced_rows(tables, message, acc, beside, total, columns):
     _, _, has = where_am_i(columns)
     for i in range(total.shape[0]):
-        total[i] = own[i] + acc[1, 0, i].astype(F32)
+        total[i] = message[tables.last_first(i)] + acc[1, 0, i].astype(F32)
     for slot, col in ((0, 0), (1, 2)):
         @pl.when(has[col])
         def _():
@@ -218,30 +302,76 @@
     return lax.broadcasted_iota(jnp.int32, shape, 0) < count
 
 
-def spread_features(columns, counts, features, near, send_sem, recv_sem):
+def halves(slots, work):
+    middle = slots // 2
+    for start, end in ((0, middle), (middle, slots)):
+        def step(slot, carry):
+            work(slot)
+            return carry
+        yield lambda: lax.fori_loop(start, end, step, 0)
+
+
+def forward_pass(columns, counts, table, features, influence, weights, mirror_t, cotangent,
+                 activated, upstream, near,
+                 mine, tiles, left, right, to_second, to_first, sent,
+                 acc, land, beside, total, tile_sem, send_sem, recv_sem, send_sem2, recv_sem2):
     _, g, _ = where_am_i(columns)
-    blocks = features.shape[0]
-    for i in range(blocks):
+    slots, kernels, width = tiles.shape[0], tiles.shape[1], features.shape[2]
+    tables = Tables(table, slots, features.shape[0])
+    for slot in range(slots):
+        fetch(influence, tiles, tile_sem, slot).start()
+    for i in range(features.shape[0]):
         rows = features[i].astype(F32)
-        near[1, g, i] = jnp.where(rows_below(counts[i], rows.shape), rows, 0.0).astype(BF16)
+        rows = jnp.where(rows_below(counts[i], rows.shape), rows, 0.0).astype(BF16)
+        mine[i] = rows
+        near[1, g, i] = rows
+    clear_edges(near, columns)
+    to_second[slots] = jnp.zeros(to_second.shape[1:], F32)
+    to_first[slots] = jnp.zeros(to_first.shape[1:], F32)
+
+    def own_terms(slot):
+        fetch(influence, tiles, tile_sem, slot).wait()
+        rows_t = mine[tables.first(slot)].astype(F32).T.astype(BF16)
+        left[...] = dot(mirror_t[...], rows_t).astype(BF16)
+        value = jnp.zeros(to_second.shape[1:][::-1], F32)
+        for k in range(kernels):
+            value += dot(left[k * width:(k + 1) * width, :], tiles[slot, k])
+        to_second[slot] = value.T + to_second[tables.before_second(slot)]
+
+    def near_terms(slot):
+        col, h, x = tables.second(slot)
+        right[...] = dot(near[col, h, x], weights[...]).astype(BF16)
+        value = jnp.zeros(to_first.shape[1:], F32)
+        for k in range(kernels):
+            value += dot(tiles[slot, k], right[:, k * width:(k + 1) * width])
+        to_first[slot] = value + to_first[tables.before_first(slot)]
+
     greet(columns, near.shape[1])
-    spread(near, send_sem, recv_sem, columns)
-
-
-def finish_forward(columns, counts, own, sent, cotangent, activated, near,
-                   acc, land, beside, total, send_sem, recv_sem, send_sem2, recv_sem2):
-    _, g, _ = where_am_i(columns)
-    greet(columns, near.shape[1])
-    run(gather_back(sent, acc, land, beside, send_sem, recv_sem, columns))
-    reduced_rows(own, acc, beside, total, columns)
+    work = halves(slots, own_terms)
+    steps = spread(near, send_sem, recv_sem, columns)
+    next(steps)
+    next(work)()
+    next(steps)
+    next(work)()
+    run(steps)
+    fill_sent(sent, tables, to_second)
+    work = halves(slots, near_terms)
+    steps = gather_back(sent, acc, land, beside, send_sem2, recv_sem2, columns)
+    next(steps)
+    next(steps)
+    next(work)()
+    next(steps)
+    next(steps)
+    next(work)()
+    run(steps)
+    reduced_rows(tables, to_first, acc, beside, total, columns)
     for i in range(total.shape[0]):
         keep = rows_below(counts[i], total.shape[1:])
         pre = jnp.where(keep, total[i], 0.0)
         sig = jax.nn.sigmoid(pre)
         activated[i] = (pre * sig).astype(BF16)
         slope = sig * (1.0 + pre * (1.0 - sig))
-        near[1, g, i] = jnp.where(keep, cotangent[i].astype(F32) * slope, 0.0).astype(BF16)
-    spread(near, send_sem2, recv_sem2, columns)
+        upstream[i] = jnp.where(keep, cotangent[i].astype(F32) * slope, 0.0).astype(BF16)
 
 
 def sum_weights(scale, terms, out, land, held, low, low_land, mixed, gathered, send_sem, recv_sem, columns):
@@ -333,88 +463,74 @@
         out[h] = gathered[h].astype(F32) * scale
 
 
-def finish_backward(scale, columns, counts, own, sent, terms, grad, summed, acc, land, beside, total, send_sem, recv_sem,
-                    w_land, w_held, w_low, w_low_land, w_mixed, w_gathered, w_send, w_recv):
-    greet(columns, sent.shape[1], True)
-    run(sum_weights(scale, terms, summed, w_land, w_held, w_low, w_low_land, w_mixed, w_gathered, w_send, w_recv, columns),
-        gather_back(sent, acc, land, beside, send_sem, recv_sem, columns))
-    reduced_rows(own, acc, beside, total, columns)
+def backward_pass(scale, columns, counts, table, near, upstream, influence, weights, mirror_t,
+                  grad, summed,
+                  near_up, tiles, up_t, up_own, grad_near, grad_own, grads, to_second, to_first, sent,
+                  acc, land, beside, total, tile_sem, send_sem, recv_sem, send_sem2, recv_sem2,
+                  w_land, w_held, w_low, w_low_land, w_mixed, w_gathered, w_send, w_recv):
+    _, g, _ = where_am_i(columns)
+    slots, kernels, width = tiles.shape[0], tiles.shape[1], upstream.shape[2]
+    tables = Tables(table, slots, upstream.shape[0])
+    for slot in range(slots):
+        fetch(influence, tiles, tile_sem, slot).start()
+    for i in range(upstream.shape[0]):
+        near_up[1, g, i] = upstream[i]
+    clear_edges(near_up, columns)
+    to_second[slots] = jnp.zeros(to_second.shape[1:], F32)
+    to_first[slots] = jnp.zeros(to_first.shape[1:], F32)
+    grad_near[...] = jnp.zeros_like(grad_near)
+    grad_own[...] = jnp.zeros_like(grad_own)
+
+    def near_terms(slot):
+        fetch(influence, tiles, tile_sem, slot).wait()
+        col, h, x = tables.second(slot)
+        up_first_t = (upstream[tables.first(slot)].astype(F32) * tables.flag(slot)).T.astype(BF16)
+        for k in range(kernels):
+            up_t[k * width:(k + 1) * width, :] = dot(up_first_t, tiles[slot, k]).astype(BF16)
+        grad_near[...] += dot(up_t[...], near[col, h, x])
+        to_second[slot] = dot(weights[...], up_t[...]).T + to_second[tables.before_second(slot)]
+
+    def own_terms(slot):
+        col, h, x = tables.second(slot)
+        up_second = (near_up[col, h, x].astype(F32) * tables.flag(slot)).astype(BF16)
+        for k in range(kernels):
+            up_own[:, k * width:(k + 1) * width] = dot(tiles[slot, k], up_second).astype(BF16)
+        rows_t = near[1, g, tables.first(slot)].astype(F32).T.astype(BF16)
+        grad_own[...] += dot(rows_t, up_own[...])
+        to_first[slot] = dot(up_own[...], mirror_t[...]) + to_first[tables.before_first(slot)]
+
+    greet(columns, near.shape[1], True)
+    work = halves(slots, near_terms)
+    steps = spread(near_up, send_sem, recv_sem, columns)
+    next(steps)
+    next(work)()
+    next(steps)
+    next(work)()
+    run(steps)
+    fill_sent(sent, tables, to_second)
+    work = halves(slots, own_terms)
+    steps = gather_back(sent, acc, land, beside, send_sem2, recv_sem2, columns)
+    next(steps)
+    next(steps)
+    next(work)()
+    next(steps)
+    next(work)()
+    rows = grads.shape[2]
+    shares = width // rows
+    for k in range(kernels):
+        mirrored = kernels - 1 - k
+        value = grad_near[k * width:(k + 1) * width, :].T + grad_own[:, mirrored * width:(mirrored + 1) * width]
+        for i in range(shares):
+            at = k * shares + i
+            grads[at // columns, at % columns] = value[i * rows:(i + 1) * rows]
+    for at in range(kernels * shares, grads.shape[0] * columns):
+        grads[at // columns, at % columns] = jnp.zeros(grads.shape[2:], F32)
+    run(sum_weights(scale, grads, summed, w_land, w_held, w_low, w_low_land, w_mixed, w_gathered, w_send, w_recv, columns),
+        steps)
+    reduced_rows(tables, to_first, acc, beside, total, columns)
     for i in range(total.shape[0]):
         keep = rows_below(counts[i], total.shape[1:])
         grad[i] = jnp.where(keep, total[i], 0.0).astype(BF16)
-
-
-def dot(a, b):
-    return jnp.dot(a, b, preferred_element_type=F32)
-
-
-def zero_blocks(ref):
-    def clear(i, carry):
-        ref[i] = jnp.zeros(ref.shape[1:], ref.dtype)
-        return carry
-    lax.fori_loop(0, ref.shape[0], clear, 0)
-
-
-def forward_slots(first_of, near_of, base, used, tile, near, weights, mirror_t, own, sent, left, right):
-    slot = pl.program_id(0)
-    kernels, width = tile.shape[1], near.shape[2]
-
-    @pl.when(slot == 0)
-    def _():
-        zero_blocks(own)
-        zero_blocks(sent)
-
-    @pl.when(slot < used[0])
-    def _():
-        first, second = first_of[slot], near_of[slot]
-        right[...] = dot(near[second], weights[...]).astype(BF16)
-        rows_t = near[base[0] + first].astype(F32).T.astype(BF16)
-        left[...] = dot(mirror_t[...], rows_t).astype(BF16)
-        to_first = jnp.zeros(own.shape[1:], F32)
-        to_second = jnp.zeros(own.shape[1:][::-1], F32)
-        for k in range(kernels):
-            cut = pl.ds(k * width, width)
-            to_first += dot(tile[0, k], right[:, cut])
-            to_second += dot(left[cut, :], tile[0, k])
-        own[first] += to_first
-        sent[second] = (sent[second].astype(F32) + to_second.T).astype(BF16)
-
-
-def backward_slots(first_of, near_of, base, used, tile, near, near_up, weights, mirror_t,
-                   own, sent, grads, grad_near, grad_own, up_t, up_own):
-    slot = pl.program_id(0)
-    kernels, width = tile.shape[1], near.shape[2]
-
-    @pl.when(slot == 0)
-    def _():
-        zero_blocks(own)
-        zero_blocks(sent)
-        grad_near[...] = jnp.zeros_like(grad_near)
-        grad_own[...] = jnp.zeros_like(grad_own)
-
-    @pl.when(slot < used[0])
-    def _():
-        first, second = first_of[slot], near_of[slot]
-        up_first_t = near_up[base[0] + first].astype(F32).T.astype(BF16)
-        up_second = near_up[second]
-        for k in range(kernels):
-            cut = pl.ds(k * width, width)
-            up_t[cut, :] = dot(up_first_t, tile[0, k]).astype(BF16)
-            up_own[:, cut] = dot(tile[0, k], up_second).astype(BF16)
-        rows_t = near[base[0] + first].astype(F32).T.astype(BF16)
-        grad_near[...] += dot(up_t[...], near[second])
-        grad_own[...] += dot(rows_t, up_own[...])
-        to_second = dot(weights[...], up_t[...])
-        own[first] += dot(up_own[...], mirror_t[...])
-        sent[second] = (sent[second].astype(F32) + to_second.T).astype(BF16)
-
-    @pl.when(slot == pl.num_programs(0) - 1)
-    def _():
-        for k in range(kernels):
-            mirrored = kernels - 1 - k
-            grads[k] = grad_near[k * width:(k + 1) * width, :].T + grad_own[:, mirrored * width:(mirrored + 1) * width]
-        for k in range(kernels, grads.shape[0]):
-            grads[k] = jnp.zeros(grads.shape[1:], F32)
 
 
 def body(features, point_counts, kernel_weights, influence, pair_list, pair_counts, cotangent):
@@ -422,23 +538,17 @@
     kernels = kernel_weights.shape[0]
     slots = influence.shape[0]
     columns, groups = lax.axis_size("block"), lax.axis_size("grp")
-    b, g = lax.axis_index("block"), lax.axis_index("grp")
-    region = groups * blocks
-    flat = (3 * region, points, width)
     spread_shape = (3, groups, blocks, points, width)
     own_shape = (blocks, points, width)
-    copies = 3 * groups * PARTS
-
-    used = pair_counts
-    first_of = pair_list[:, 0]
-    near_of = pair_list[:, 1] - (b - 1) * region
-    base = (region + g * blocks).astype(jnp.int32)[None]
+    terms = (kernels * width, points)
+
+    table = table_of(pair_list, pair_counts[0], lax.axis_index("block"), blocks, groups)
     weights = kernel_weights.transpose(1, 0, 2).reshape(width, kernels * width)
     mirror_t = kernel_weights[::-1].transpose(0, 2, 1).reshape(kernels * width, width)
 
     def remote(kernel, collective, ins, outs, scratch, args):
         return pl.pallas_call(
-            functools.partial(kernel, columns),
+            kernel,
             in_specs=ins,
             out_specs=[VMEM] * len(outs),
             out_shape=outs,
@@ -447,59 +557,38 @@
                 collective_id=collective, has_side_effects=True, vmem_limit_bytes=VMEM_BYTES),
         )(*args)
 
-    dma = pltpu.SemaphoreType.DMA((copies,))
-    reduce_scratch = [
+    hbm = pl.BlockSpec(memory_space=pl.ANY)
+    dma = pltpu.SemaphoreType.DMA((3 * groups * PARTS,))
+    messages = pltpu.VMEM((slots + 1, points, width), F32)
+    tiles = pltpu.VMEM(influence.shape, BF16)
+    exchange = [
+        messages, messages, pltpu.VMEM(spread_shape, BF16),
         pltpu.VMEM(spread_shape, BF16), pltpu.VMEM(spread_shape, BF16),
-        pltpu.VMEM((2, *own_shape), BF16), pltpu.VMEM(own_shape, F32), dma, dma]
+        pltpu.VMEM((2, *own_shape), BF16), pltpu.VMEM(own_shape, F32),
+        pltpu.SemaphoreType.DMA((slots,)), dma, dma, dma, dma]
     near_type = jax.ShapeDtypeStruct(spread_shape, BF16)
     own_type = jax.ShapeDtypeStruct(own_shape, BF16)
 
-    def tile_at(slot, first_of, near_of, base, used):
-        return (jnp.minimum(slot, used[0] - 1), 0, 0, 0)
-
-    def fixed(shape):
-        return pl.BlockSpec(shape, lambda slot, *_: (0,) * len(shape))
-
-    def local(kernel, ins, outs, scratch, args):
-        return pl.pallas_call(
-            kernel,
-            grid_spec=pltpu.PrefetchScalarGridSpec(
-                num_scalar_prefetch=4, grid=(slots,),
-                in_specs=[pl.BlockSpec((1, kernels, points, points), tile_at)] + [fixed(a.shape) for a in ins],
-                out_specs=[fixed(a.shape) for a in outs],
-                scratch_shapes=scratch),
-            out_shape=outs,
-            compiler_params=pltpu.CompilerParams(vmem_limit_bytes=VMEM_BYTES),
-        )(first_of, near_of, base, used, influence, *args)
-
-    (near,) = remote(spread_features, 0, [SMEM, VMEM], [near_type], [dma, dma], (point_counts, features))
-    near_rows = near.reshape(flat)
-    slot_outs = [jax.ShapeDtypeStruct(own_shape, F32), jax.ShapeDtypeStruct(flat, BF16)]
-    ins = (near_rows, weights, mirror_t)
-    own, sent = local(
-        forward_slots, ins, slot_outs,
-        [pltpu.VMEM((kernels * width, points), BF16), pltpu.VMEM((points, kernels * width), BF16)], ins)
-    activated, near_up = remote(
-        finish_forward, 1, [SMEM, VMEM, VMEM, VMEM], [own_type, near_type],
-        reduce_scratch + [dma, dma],
-        (point_counts, own, sent.reshape(spread_shape), cotangent))
-    ins = (near_rows, near_up.reshape(flat), weights, mirror_t)
+    activated, upstream, near = remote(
+        functools.partial(forward_pass, columns), 0,
+        [SMEM, SMEM, VMEM, hbm, VMEM, VMEM, VMEM], [own_type, own_type, near_type],
+        [pltpu.VMEM(own_shape, BF16), tiles, pltpu.VMEM(terms, BF16), pltpu.VMEM(terms[::-1], BF16)] + exchange,
+        (point_counts, table, features, influence, weights, mirror_t, cotangent))
+
+    scale = 1.0 / math.sqrt(blocks * points * columns * groups)
     share = 16 * columns * groups
     padded = -(-kernels * width // share) * share // width
-    own, sent, grads = local(
-        backward_slots, ins, slot_outs + [jax.ShapeDtypeStruct((padded, width, width), F32)],
-        [pltpu.VMEM((kernels * width, width), F32), pltpu.VMEM((width, kernels * width), F32),
-         pltpu.VMEM((kernels * width, points), BF16), pltpu.VMEM((points, kernels * width), BF16)], ins)
-    scale = 1.0 / math.sqrt(blocks * points * columns * groups)
     cut = (groups, columns, padded * width // (groups * columns), width)
     w_dma = pltpu.SemaphoreType.DMA((2 * groups + 2 * columns,))
     grad_features, summed = remote(
-        functools.partial(finish_backward, scale), 2, [SMEM, VMEM, VMEM, VMEM],
-        [own_type, jax.ShapeDtypeStruct(cut, F32)],
-        reduce_scratch + [
+        functools.partial(backward_pass, scale, columns), 1,
+        [SMEM, SMEM, VMEM, VMEM, hbm, VMEM, VMEM], [own_type, jax.ShapeDtypeStruct(cut, F32)],
+        [pltpu.VMEM(spread_shape, BF16), tiles, pltpu.VMEM(terms, BF16), pltpu.VMEM(terms[::-1], BF16),
+         pltpu.VMEM((kernels * width, width), F32), pltpu.VMEM((width, kernels * width), F32), pltpu.VMEM(cut, F32)]
+        + exchange + [
             pltpu.VMEM(cut, F32), pltpu.VMEM(cut, F32), pltpu.VMEM(cut, BF16), pltpu.VMEM(cut, BF16),
             pltpu.VMEM(cut[1:], BF16), pltpu.VMEM(cut, BF16), w_dma, w_dma],
-        (point_counts, own, sent.reshape(spread_shape), grads.reshape(cut)))
+        (point_counts, table, near, upstream, influence, weights, mirror_t))
     grad_weights = summed.reshape(padded, width, width)[:kernels]
     return (activated, grad_features, grad_weights)
 

time: 161 us -> 136 us (0.84)
  Pallas kernels: 149 us -> 122 us
    pallas_call x5 -> x2, Pallas kernels: 149 us -> 122 us  [remote(): pl.pallas_call(kernel, in_specs=ins, out_specs=[VMEM] * len(outs), out_sh...]
where the time goes in v3:
time: 136 us; the launch traced here: 135 us
  Pallas kernels  122 us (90%)
  local copies, waits for them, and re-layouts  9.56 us (7%)
  other arithmetic  2.63 us (2%)
    pallas_call x2, Pallas kernels, remote(): pl.pallas_call(kernel, in_specs=ins, out_specs=[VMEM] * len(outs), out_sh...  122 us
    unnamed x5, local copies, waits for them, and re-layouts  3.67 us

profile of v3, /device:TPU:0, one launch (start us, length us, event | category | flops | bytes accessed | tf_op | source)
XLA Modules:
  0.0 135.2 jit_solution(17254840746408942867)
XLA Ops:
  1.3 0.7 and_select_fusion.4
  2.0 0.8 fusion.6
  2.8 0.1 select_reduce_fusion.3
  2.9 0.7 multiply_add_fusion
  3.6 0.1 select_reduce_fusion
  3.7 0.2 select_reduce_fusion.1
  3.9 0.6 concatenate.3.table
  4.5 1.1 reverse_bitcast_fusion
  5.6 1.0 copy.17
  6.6 1.3 copy.16
  7.9 1.0 copy.18.weights
  8.9 51.5 %shard_map.94 = (bf16[4,256,128]{2,1,0:T(8,128)(2,1)}, bf16[4,256,128]{2,1,0:T(8,128)(2,1)}, bf16[3,4,4,256,128]{4,3,2,1,0:T(8,128)(2,1)}) custom-call(s32[4]{0:T(128)} %counts.3, s32[108]{0:T(128)} %concatenate.3.table, bf16[4,256,128]{2,1,0:T(8,128)(2,1)} %features.1, bf16[8,15,256,256]{3,2,1,0:T(8,128)(2,1)} %influence.3, ...), custom_call_target="tpu_custom_call" | custom-call | tf_op jit(solution)/shard_map/pallas_call | solution.py:550
  60.4 0.0 copy-start
  60.4 70.2 %shard_map.95 = (bf16[4,256,128]{2,1,0:T(8,128)(2,1)}, f32[4,8,64,128]{3,2,1,0:T(8,128)}) custom-call(s32[4]{0:T(128)} %counts.3, s32[108]{0:T(128)} %concatenate.3.table, bf16[3,4,4,256,128]{4,3,2,1,0:T(8,128)(2,1)} %get-tuple-element.9.near, bf16[4,256,128]{2,1,0:T(8,128)(2,1)} %get-tuple-element.10.upstream, bf16[8,15,256,256]{3,2,1,0:T(8,128)(2,1)} %influence.3, ...), custom_call_target="tpu_custom_call" | custom-call | tf_op jit(solution)/shard_map/pallas_call | solution.py:550
  130.6 2.2 %slice.13 = f32[15,128,128]{2,1,0:T(8,128)} slice(f32[16,128,128]{2,1,0:T(8,128)} %bitcast.28), slice={[0:15], [0:128], [0:128]} | slice | bytes 1966080 | tf_op jit(solution)/shard_map/slice | solution.py:592
  132.8 0.0 copy-done
  132.8 0.7 copy.23
  133.5 1.7 %copy.24 = bf16[4,256,128]{2,1,0:T(8,128)(2,1)} copy(bf16[4,256,128]{2,1,0:T(8,128)(2,1)} %get-tuple-element.28) | data formatting | bytes 524288
  (5 shorter events, 0.0 us)
Async XLA Ops:
  60.4 72.4 %copy-start = (bf16[4,256,128]{2,1,0:T(8,128)(2,1)S(1)}, bf16[4,256,128]{2,1,0:T(8,128)(2,1)}, u32[]{:S(2)}) copy-start(bf16[4,256,128]{2,1,0:T(8,128)(2,1)} %get-tuple-element.27) | copy-start | bytes 786436

commit v4 on v3

--- a/solution.py
+++ b/solution.py
@@ -177,22 +177,36 @@
             for col in cols:
                 under(has[col], lambda: grp_copy(col, mask, part).start())
     yield
+    held_back = []
     for bit in reversed(grp_bits(groups)):
         kept = [m for m in range(groups) if m % (2 * bit) == 0]
+
+        def settle(mask, col, part):
+            def step():
+                grp_copy(col, mask | bit, part).wait_recv()
+                held = sent.at[col, g ^ mask, cut(part)] if bit == 1 else acc.at[col, mask, cut(part)]
+                add_blocks(acc.at[col, mask, cut(part)], held, land.at[col, mask | bit, cut(part)], span)
+                if mask and low_bit(mask) == 2 * bit:
+                    if col == 1 and 4 * bit == groups:
+                        held_back.append((mask, part))
+                    else:
+                        grp_copy(col, mask, part).start()
+                if 2 * bit == groups and col != 1:
+                    side_copy(col, part).start()
+            under(has[col], step)
+
         for mask in sorted(kept, reverse=True):
             for part in parts:
-                for col in cols:
-                    def step():
-                        grp_copy(col, mask | bit, part).wait_recv()
-                        held = sent.at[col, g ^ mask, cut(part)] if bit == 1 else acc.at[col, mask, cut(part)]
-                        add_blocks(acc.at[col, mask, cut(part)], held, land.at[col, mask | bit, cut(part)], span)
-                        if mask and low_bit(mask) == 2 * bit:
-                            grp_copy(col, mask, part).start()
-                        if 2 * bit == groups and col != 1:
-                            side_copy(col, part).start()
-                    under(has[col], step)
+                for col in (0, 2):
+                    settle(mask, col, part)
                 if 2 * bit == groups and part == PARTS // 2 - 1:
                     yield
+                    for late, piece in held_back:
+                        grp_copy(1, late, piece).start()
+            if 2 * bit == groups:
+                yield
+            for part in parts:
+                settle(mask, 1, part)
             yield
     for part in parts:
         for col in (0, 2):
@@ -302,6 +316,13 @@
     return lax.broadcasted_iota(jnp.int32, shape, 0) < count
 
 
+def lay_out(kernel_weights, weights, mirror_t):
+    kernels, width = kernel_weights.shape[:2]
+    for k in range(kernels):
+        weights[:, k * width:(k + 1) * width] = kernel_weights[k]
+        mirror_t[k * width:(k + 1) * width, :] = kernel_weights[kernels - 1 - k].astype(F32).T.astype(BF16)
+
+
 def halves(slots, work):
     middle = slots // 2
     for start, end in ((0, middle), (middle, slots)):
@@ -311,9 +332,9 @@
         yield lambda: lax.fori_loop(start, end, step, 0)
 
 
-def forward_pass(columns, counts, table, features, influence, weights, mirror_t, cotangent,
+def forward_pass(columns, counts, table, features, influence, kernel_weights, cotangent,
                  activated, upstream, near,
-                 mine, tiles, left, right, to_second, to_first, sent,
+                 weights, mirror_t, mine, tiles, left, right, to_second, to_first, sent,
                  acc, land, beside, total, tile_sem, send_sem, recv_sem, send_sem2, recv_sem2):
     _, g, _ = where_am_i(columns)
     slots, kernels, width = tiles.shape[0], tiles.shape[1], features.shape[2]
@@ -325,6 +346,7 @@
         rows = jnp.where(rows_below(counts[i], rows.shape), rows, 0.0).astype(BF16)
         mine[i] = rows
         near[1, g, i] = rows
+    lay_out(kernel_weights, weights, mirror_t)
     clear_edges(near, columns)
     to_second[slots] = jnp.zeros(to_second.shape[1:], F32)
     to_first[slots] = jnp.zeros(to_first.shape[1:], F32)
@@ -359,8 +381,8 @@
     steps = gather_back(sent, acc, land, beside, send_sem2, recv_sem2, columns)
     next(steps)
     next(steps)
-    next(work)()
-    next(steps)
+    next(steps)
+    next(work)()
     next(steps)
     next(work)()
     run(steps)
@@ -459,13 +481,16 @@
     for distance in distances:
         share(distance).wait_send()
         tell(distance).wait_send()
-    for h in range(groups):
-        out[h] = gathered[h].astype(F32) * scale
-
-
-def backward_pass(scale, columns, counts, table, near, upstream, influence, weights, mirror_t,
+    rows = gathered.shape[2]
+    shares = out.shape[1] // rows
+    for at in range(out.shape[0] * shares):
+        piece = gathered[at // columns, at % columns]
+        out[at // shares, at % shares * rows:(at % shares + 1) * rows] = piece.astype(F32) * scale
+
+
+def backward_pass(scale, columns, counts, table, near, upstream, influence, kernel_weights,
                   grad, summed,
-                  near_up, tiles, up_t, up_own, grad_near, grad_own, grads, to_second, to_first, sent,
+                  weights, mirror_t, near_up, tiles, up_t, up_own, grad_near, grad_own, grads, to_second, to_first, sent,
                   acc, land, beside, total, tile_sem, send_sem, recv_sem, send_sem2, recv_sem2,
                   w_land, w_held, w_low, w_low_land, w_mixed, w_gathered, w_send, w_recv):
     _, g, _ = where_am_i(columns)
@@ -475,6 +500,7 @@
         fetch(influence, tiles, tile_sem, slot).start()
     for i in range(upstream.shape[0]):
         near_up[1, g, i] = upstream[i]
+    lay_out(kernel_weights, weights, mirror_t)
     clear_edges(near_up, columns)
     to_second[slots] = jnp.zeros(to_second.shape[1:], F32)
     to_first[slots] = jnp.zeros(to_first.shape[1:], F32)
@@ -513,6 +539,7 @@
     next(steps)
     next(steps)
     next(work)()
+    next(steps)
     next(steps)
     next(work)()
     rows = grads.shape[2]
@@ -525,12 +552,21 @@
             grads[at // columns, at % columns] = value[i * rows:(i + 1) * rows]
     for at in range(kernels * shares, grads.shape[0] * columns):
         grads[at // columns, at % columns] = jnp.zeros(grads.shape[2:], F32)
-    run(sum_weights(scale, grads, summed, w_land, w_held, w_low, w_low_land, w_mixed, w_gathered, w_send, w_recv, columns),
-        steps)
+    weight_steps = sum_weights(
+        scale, grads, summed, w_land, w_held, w_low, w_low_land, w_mixed, w_gathered, w_send, w_recv, columns)
+    next(weight_steps)
+    next(weight_steps)
+    next(steps)
+    next(weight_steps)
+    next(steps)
+    next(weight_steps)
+    run(steps)
+    next(weight_steps)
     reduced_rows(tables, to_first, acc, beside, total, columns)
     for i in range(total.shape[0]):
         keep = rows_below(counts[i], total.shape[1:])
         grad[i] = jnp.where(keep, total[i], 0.0).astype(BF16)
+    run(weight_steps)
 
 
 def body(features, point_counts, kernel_weights, influence, pair_list, pair_counts, cotangent):
@@ -543,8 +579,6 @@
     terms = (kernels * width, points)
 
     table = table_of(pair_list, pair_counts[0], lax.axis_index("block"), blocks, groups)
-    weights = kernel_weights.transpose(1, 0, 2).reshape(width, kernels * width)
-    mirror_t = kernel_weights[::-1].transpose(0, 2, 1).reshape(kernels * width, width)
 
     def remote(kernel, collective, ins, outs, scratch, args):
         return pl.pallas_call(
@@ -566,30 +600,30 @@
         pltpu.VMEM(spread_shape, BF16), pltpu.VMEM(spread_shape, BF16),
         pltpu.VMEM((2, *own_shape), BF16), pltpu.VMEM(own_shape, F32),
         pltpu.SemaphoreType.DMA((slots,)), dma, dma, dma, dma]
+    laid_out = [pltpu.VMEM((width, kernels * width), BF16), pltpu.VMEM((kernels * width, width), BF16)]
     near_type = jax.ShapeDtypeStruct(spread_shape, BF16)
     own_type = jax.ShapeDtypeStruct(own_shape, BF16)
 
     activated, upstream, near = remote(
         functools.partial(forward_pass, columns), 0,
-        [SMEM, SMEM, VMEM, hbm, VMEM, VMEM, VMEM], [own_type, own_type, near_type],
-        [pltpu.VMEM(own_shape, BF16), tiles, pltpu.VMEM(terms, BF16), pltpu.VMEM(terms[::-1], BF16)] + exchange,
-        (point_counts, table, features, influence, weights, mirror_t, cotangent))
+        [SMEM, SMEM, VMEM, hbm, VMEM, VMEM], [own_type, own_type, near_type],
+        laid_out + [pltpu.VMEM(own_shape, BF16), tiles, pltpu.VMEM(terms, BF16), pltpu.VMEM(terms[::-1], BF16)] + exchange,
+        (point_counts, table, features, influence, kernel_weights, cotangent))
 
     scale = 1.0 / math.sqrt(blocks * points * columns * groups)
     share = 16 * columns * groups
     padded = -(-kernels * width // share) * share // width
     cut = (groups, columns, padded * width // (groups * columns), width)
     w_dma = pltpu.SemaphoreType.DMA((2 * groups + 2 * columns,))
-    grad_features, summed = remote(
+    grad_features, grad_weights = remote(
         functools.partial(backward_pass, scale, columns), 1,
-        [SMEM, SMEM, VMEM, VMEM, hbm, VMEM, VMEM], [own_type, jax.ShapeDtypeStruct(cut, F32)],
-        [pltpu.VMEM(spread_shape, BF16), tiles, pltpu.VMEM(terms, BF16), pltpu.VMEM(terms[::-1], BF16),
+        [SMEM, SMEM, VMEM, VMEM, hbm, VMEM], [own_type, jax.ShapeDtypeStruct(kernel_weights.shape, F32)],
+        laid_out + [pltpu.VMEM(spread_shape, BF16), tiles, pltpu.VMEM(terms, BF16), pltpu.VMEM(terms[::-1], BF16),
          pltpu.VMEM((kernels * width, width), F32), pltpu.VMEM((width, kernels * width), F32), pltpu.VMEM(cut, F32)]
         + exchange + [
             pltpu.VMEM(cut, F32), pltpu.VMEM(cut, F32), pltpu.VMEM(cut, BF16), pltpu.VMEM(cut, BF16),
             pltpu.VMEM(cut[1:], BF16), pltpu.VMEM(cut, BF16), w_dma, w_dma],
-        (point_counts, table, near, upstream, influence, weights, mirror_t))
-    grad_weights = summed.reshape(padded, width, width)[:kernels]
+        (point_counts, table, near, upstream, influence, kernel_weights))
     return (activated, grad_features, grad_weights)
 
 

time: 136 us -> 126 us (0.926)
  Pallas kernels: 122 us -> 117 us
  local copies, waits for them, and re-layouts: 9.56 us -> 5.21 us
    pallas_call x2, Pallas kernels: 122 us -> 117 us  [remote(): pl.pallas_call(kernel, in_specs=ins, out_specs=[VMEM] * len(outs), out_sh...]
    slice x1 -> x0, local copies, waits for them, and re-layouts: 2.23 us -> none  [body(): grad_weights = summed.reshape(padded, width, width)[:kernels]]
    transpose x2 -> x0, local copies, waits for them, and re-layouts: 2.05 us -> none  [body(): kernel_weights[::-1].transpose(0, 2, 1).reshape(kernels * width, width)]
where the time goes in v4:
time: 126 us
  Pallas kernels  117 us (93%)
  local copies, waits for them, and re-layouts  5.21 us (4%)
  other arithmetic  2.63 us (2%)
  between operations  1.35 us (1%)
    pallas_call x2, Pallas kernels, remote(): pl.pallas_call(kernel, in_specs=ins, out_specs=[VMEM] * len(outs), out_sh...  117 us
    unnamed x5, local copies, waits for them, and re-layouts  4.61 us

profile of v4, /device:TPU:0, one launch (start us, length us, event | category | flops | bytes accessed | tf_op | source)
XLA Modules:
  0.0 125.9 jit_solution(16205288760647919792)
XLA Ops:
  1.3 0.7 and_select_fusion.4
  2.0 0.8 fusion.6
  2.8 0.1 select_reduce_fusion.3
  2.9 0.7 multiply_add_fusion
  3.6 0.1 select_reduce_fusion
  3.7 0.2 select_reduce_fusion.1
  3.9 0.6 concatenate.3.table
  4.5 47.5 %shard_map.94 = (bf16[4,256,128]{2,1,0:T(8,128)(2,1)}, bf16[4,256,128]{2,1,0:T(8,128)(2,1)}, bf16[3,4,4,256,128]{4,3,2,1,0:T(8,128)(2,1)}) custom-call(s32[4]{0:T(128)} %counts.3, s32[108]{0:T(128)} %concatenate.3.table, bf16[4,256,128]{2,1,0:T(8,128)(2,1)} %features.1, bf16[8,15,256,256]{3,2,1,0:T(8,128)(2,1)} %influence.3, ...), custom_call_target="tpu_custom_call" | custom-call | tf_op jit(solution)/shard_map/pallas_call | solution.py:584
  52.1 0.0 copy-start
  52.1 69.2 %shard_map.95 = (bf16[4,256,128]{2,1,0:T(8,128)(2,1)}, f32[15,128,128]{2,1,0:T(8,128)}) custom-call(s32[4]{0:T(128)} %counts.3, s32[108]{0:T(128)} %concatenate.3.table, bf16[3,4,4,256,128]{4,3,2,1,0:T(8,128)(2,1)} %get-tuple-element.9.near, bf16[4,256,128]{2,1,0:T(8,128)(2,1)} %get-tuple-element.10.upstream, bf16[8,15,256,256]{3,2,1,0:T(8,128)(2,1)} %influence.3, ...), custom_call_target="tpu_custom_call" | custom-call | tf_op jit(solution)/shard_map/pallas_call | solution.py:584
  121.3 0.0 copy-done
  121.3 0.7 copy.14
  122.0 1.7 %copy.15 = bf16[4,256,128]{2,1,0:T(8,128)(2,1)} copy(bf16[4,256,128]{2,1,0:T(8,128)(2,1)} %get-tuple-element.28) | data formatting | bytes 524288
  123.7 2.2 %copy.16 = f32[15,128,128]{2,1,0:T(8,128)} copy(f32[15,128,128]{2,1,0:T(8,128)} %get-tuple-element.29) | data formatting | bytes 1966080
  (5 shorter events, 0.0 us)
Async XLA Ops:
  52.1 69.2 %copy-start = (bf16[4,256,128]{2,1,0:T(8,128)(2,1)S(1)}, bf16[4,256,128]{2,1,0:T(8,128)(2,1)}, u32[]{:S(2)}) copy-start(bf16[4,256,128]{2,1,0:T(8,128)(2,1)} %get-tuple-element.27) | copy-start | bytes 786436

commit v5 on v4

--- a/solution.py
+++ b/solution.py
@@ -72,11 +72,11 @@
     def sem(col, mask, part):
         return (col * groups + mask) * PARTS + part
 
-    def side_copy(col, part):
-        i = sem(col, 0, part)
+    def side_copy(col, part, mask=0):
+        i = sem(col, mask, part)
         step = 1 if col == 0 else -1
         return pltpu.make_async_remote_copy(
-            src_ref=at(1, 0, part), dst_ref=at(col, 0, part), send_sem=send_sem.at[i],
+            src_ref=at(1, mask, part), dst_ref=at(col, mask, part), send_sem=send_sem.at[i],
             recv_sem=recv_sem.at[i], device_id=(b + step, g), device_id_type=MESH)
 
     def grp_copy(col, mask, part):
@@ -93,17 +93,29 @@
             src_ref=at(col, mask ^ bit, part), dst_ref=at(col, mask, part), send_sem=send_sem.at[i],
             recv_sem=recv_sem.at[i], device_id=(b, g ^ bit), device_id_type=MESH)
 
+    top, turned = groups // 2, PARTS - 1
+
+    def detour(col, mask, part):
+        return col != 1 and mask == top and part == turned
+
     def forward(col, mask, part):
         for bit in grp_bits(groups):
-            if mask == 0 or bit < low_bit(mask):
+            if (mask == 0 or bit < low_bit(mask)) and not detour(col, mask | bit, part):
                 grp_copy(col, mask | bit, part).start()
 
     parts = range(PARTS)
+    forward(1, 0, turned)
     for part in parts:
         for col in (0, 2):
             pl.when(has[opposite[col]])(lambda: side_copy(col, part).start())
-        forward(1, 0, part)
+        if part != turned:
+            forward(1, 0, part)
     yield
+    if top:
+        arrival(1, top, turned).wait_recv()
+        for col in (0, 2):
+            pl.when(has[opposite[col]])(lambda: side_copy(col, turned, top).start())
+        forward(1, top, turned)
     for part in parts:
         for col in (0, 2):
             @pl.when(has[col])
@@ -116,16 +128,23 @@
         for part in parts:
             for col in (1, 0, 2):
                 def step():
-                    arrival(col, mask, part).wait_recv()
+                    if detour(col, mask, part):
+                        side_copy(col, part, mask).wait_recv()
+                    else:
+                        arrival(col, mask, part).wait_recv()
                     forward(col, mask, part)
-                under(has[col], step)
+                if (col, mask, part) != (1, top, turned):
+                    under(has[col], step)
     for part in parts:
         for col in (0, 2):
             pl.when(has[opposite[col]])(lambda: side_copy(col, part).wait_send())
     for mask in masks:
         for part in parts:
             for col in (0, 1, 2):
-                under(has[col], lambda: grp_copy(col, mask, part).wait_send())
+                if detour(col, mask, part):
+                    pl.when(has[opposite[col]])(lambda: side_copy(col, part, mask).wait_send())
+                else:
+                    under(has[col], lambda: grp_copy(col, mask, part).wait_send())
 
 
 def run(*steps):

time: 126 us -> 124 us (0.984)
  Pallas kernels: 117 us -> 115 us
    pallas_call x2, Pallas kernels: 117 us -> 115 us  [remote(): pl.pallas_call(kernel, in_specs=ins, out_specs=[VMEM] * len(outs), out_sh...]
where the time goes in v5:
time: 124 us
  Pallas kernels  115 us (93%)
  local copies, waits for them, and re-layouts  5.21 us (4%)
  other arithmetic  2.63 us (2%)
  between operations  1.35 us (1%)
    pallas_call x2, Pallas kernels, remote(): pl.pallas_call(kernel, in_specs=ins, out_specs=[VMEM] * len(outs), out_sh...  115 us
    unnamed x5, local copies, waits for them, and re-layouts  4.61 us

profile of v5, /device:TPU:0, one launch (start us, length us, event | category | flops | bytes accessed | tf_op | source)
XLA Modules:
  0.0 123.8 jit_solution(5869156201209800043)
XLA Ops:
  1.3 0.7 and_select_fusion.4
  2.0 0.8 fusion.6
  2.8 0.1 select_reduce_fusion.3
  2.9 0.7 multiply_add_fusion
  3.6 0.1 select_reduce_fusion
  3.7 0.2 select_reduce_fusion.1
  3.9 0.6 concatenate.3.table
  4.5 46.7 %shard_map.94 = (bf16[4,256,128]{2,1,0:T(8,128)(2,1)}, bf16[4,256,128]{2,1,0:T(8,128)(2,1)}, bf16[3,4,4,256,128]{4,3,2,1,0:T(8,128)(2,1)}) custom-call(s32[4]{0:T(128)} %counts.3, s32[108]{0:T(128)} %concatenate.3.table, bf16[4,256,128]{2,1,0:T(8,128)(2,1)} %features.1, bf16[8,15,256,256]{3,2,1,0:T(8,128)(2,1)} %influence.3, ...), custom_call_target="tpu_custom_call" | custom-call | tf_op jit(solution)/shard_map/pallas_call | solution.py:603
  51.2 0.0 copy-start
  51.3 67.9 %shard_map.95 = (bf16[4,256,128]{2,1,0:T(8,128)(2,1)}, f32[15,128,128]{2,1,0:T(8,128)}) custom-call(s32[4]{0:T(128)} %counts.3, s32[108]{0:T(128)} %concatenate.3.table, bf16[3,4,4,256,128]{4,3,2,1,0:T(8,128)(2,1)} %get-tuple-element.9.near, bf16[4,256,128]{2,1,0:T(8,128)(2,1)} %get-tuple-element.10.upstream, bf16[8,15,256,256]{3,2,1,0:T(8,128)(2,1)} %influence.3, ...), custom_call_target="tpu_custom_call" | custom-call | tf_op jit(solution)/shard_map/pallas_call | solution.py:603
  119.2 0.0 copy-done
  119.2 0.7 copy.14
  119.9 1.7 %copy.15 = bf16[4,256,128]{2,1,0:T(8,128)(2,1)} copy(bf16[4,256,128]{2,1,0:T(8,128)(2,1)} %get-tuple-element.28) | data formatting | bytes 524288
  121.5 2.2 %copy.16 = f32[15,128,128]{2,1,0:T(8,128)} copy(f32[15,128,128]{2,1,0:T(8,128)} %get-tuple-element.29) | data formatting | bytes 1966080
  (5 shorter events, 0.0 us)
Async XLA Ops:
  51.2 67.9 %copy-start = (bf16[4,256,128]{2,1,0:T(8,128)(2,1)S(1)}, bf16[4,256,128]{2,1,0:T(8,128)(2,1)}, u32[]{:S(2)}) copy-start(bf16[4,256,128]{2,1,0:T(8,128)(2,1)} %get-tuple-element.27) | copy-start | bytes 786436
